TPU v7x, 128 devices: a whole 4x4x4 slice. The times are simulated.
128 devices in a mesh: row: 64 (over y, z, x), rep: 2 (over core).
Axes of the slice: x: 4, y: 4, z: 4, core: 2. Of those that a mesh axis runs over, the one named last changes fastest.
Arguments:
- node_feats: bfloat16 [131072, 256], P('row')
- out_grad: bfloat16 [131072, 256], P('row'), may hold values from -6 to 6
- mask_bits: int32 [131072, 16], P('row'), may hold values from 0 to 65535
- weight: bfloat16 [256, 256], replicated, may hold values from -0.375 to 0.375
- send_rows: int32 [64, 64, 128], P('row'), may hold values from -1 to 2047, as said below
- tile_vals: bfloat16 [64, 2, 512, 128, 128], P('row', 'rep'), may hold values from -0.0625 to 0.0625
- tile_row: int32 [64, 2, 512], P('row', 'rep'), may hold values from -1 to 15, as said below
- tile_peer: int32 [64, 2, 512], P('row', 'rep'), may hold values from 0 to 63
Outputs:
- in_grad: bfloat16 [131072, 256], P('row')
- w_grad: float32 [256, 256], replicated
Inputs may be any that keep to these rules, and one draw needn't show every extreme that they name: `send_rows`: empty slots (-1) follow the filled ones; the list from a block to itself is full and the list from block p to block p + 1 (cyclically) holds 32 rows. `tile_row`: empty slots (-1) follow the filled ones; a device's filled slots number 512, 256, 128 or 64, and device 0 of both axes has all 512.
All inputs are finite; a program needn't handle non-finite values.
Results may differ from a plain program's by a relative error of at most 0.0049.
Values may be sent and summed in bfloat16 or wider, within the bound.
A program may use at most 128 MiB of HBM per device.

v0:
```python
import math

import jax
import jax.numpy as jnp
from jax import lax
from jax.sharding import PartitionSpec as P


def unpack_mask(mask_bits):
    shifts = jnp.arange(16, dtype=jnp.int32)
    bits = jnp.bitwise_and(jnp.right_shift(mask_bits[:, :, None], shifts[None, None, :]), 1)
    return bits.reshape(mask_bits.shape[0], mask_bits.shape[1] * 16)


def local(node_feats, out_grad, mask_bits, weight, send_rows, tile_vals, tile_row, tile_peer):
    rows_here = node_feats.shape[0]
    width = node_feats.shape[1]
    mask = unpack_mask(mask_bits)
    grad_pre = jnp.where(mask == 1, out_grad, jnp.zeros_like(out_grad))
    listed = send_rows[0]
    safe = jnp.clip(listed, 0, rows_here - 1)
    picked = jnp.take(grad_pre, safe.reshape(-1), axis=0).reshape(listed.shape + (width,))
    picked = jnp.where(listed[:, :, None] >= 0, picked, jnp.zeros_like(picked))
    received = lax.all_to_all(picked, "row", split_axis=0, concat_axis=0, tiled=True)
    values = tile_vals[0, 0]
    rows = tile_row[0, 0]
    peers = tile_peer[0, 0]
    slots = values.shape[0]
    tile = values.shape[1]
    block = min(32, slots)
    row_tiles = rows_here // tile
    sources_all = received.shape[0]
    flat_received = received.reshape(sources_all, tile * width)
    peer_ids = jnp.arange(sources_all, dtype=jnp.int32)
    tile_ids = jnp.arange(row_tiles, dtype=jnp.int32)
    live_count = jnp.sum((rows >= 0).astype(jnp.int32))
    block_count = (live_count + block - 1) // block

    def add_block(index, total):
        block_vals = lax.dynamic_slice_in_dim(values, index * block, block, 0)
        block_rows = lax.dynamic_slice_in_dim(rows, index * block, block, 0)
        block_peers = lax.dynamic_slice_in_dim(peers, index * block, block, 0)
        peer_hot = (block_peers[:, None] == peer_ids[None, :]).astype(jnp.bfloat16)
        sources = jnp.dot(peer_hot, flat_received, preferred_element_type=jnp.float32)
        sources = sources.astype(jnp.bfloat16).reshape(block, tile, width)
        prods = jnp.einsum("kab,kbf->kaf", block_vals, sources, preferred_element_type=jnp.float32)
        row_hot = (tile_ids[:, None] == block_rows[None, :]).astype(jnp.float32)
        added = jnp.dot(
            row_hot,
            prods.reshape(block, tile * width),
            precision=lax.Precision.HIGHEST,
            preferred_element_type=jnp.float32,
        )
        return total + added

    start = jnp.zeros((row_tiles, tile * width), jnp.float32)
    partial_value = lax.fori_loop(0, block_count, add_block, start).reshape(rows_here, width)
    scale = 1.0 / math.sqrt(rows_here * lax.axis_size("row"))
    agg = lax.psum(partial_value, "rep").astype(jnp.bfloat16)
    in_grad = lax.dot_general(
        agg, weight, (((1,), (1,)), ((), ())), preferred_element_type=jnp.float32
    ).astype(jnp.bfloat16)
    w_term = lax.dot_general(
        node_feats, agg, (((0,), (0,)), ((), ())), preferred_element_type=jnp.float32
    )
    w_sum = lax.psum(w_term, "row")
    w_grad = w_sum * jnp.float32(scale)
    return (in_grad, w_grad)


def solution(mesh):
    placed = (
        P("row", None),
        P("row", None),
        P("row", None),
        P(),
        P("row", None, None),
        P("row", "rep", None, None, None),
        P("row", "rep", None),
        P("row", "rep", None),
    )
    return jax.shard_map(
        local, mesh=mesh, in_specs=placed, out_specs=(P("row", None), P()), check_vma=False
    )
```

profile of v0, /device:TPU:1, one launch (start us, length us, event | category | flops | bytes accessed | tf_op | source)
XLA Modules:
  0.0 453.0 jit_solution(8053174147611066499)
XLA Ops:
  7.2 0.9 compare_and_fusion
  9.7 1.1 shift_right_arithmetic.20
  10.9 1.9 copy.12
  12.7 2.3 fusion.9
  15.0 33.1 %gather_fusion = bf16[8192,256]{1,0:T(8,128)(2,1)} fusion(bf16[2048,256]{1,0:T(8,128)(2,1)S(1)} %fusion.9, s32[8192]{0:T(1024)S(1)} %broadcast_clamp_fusion), kind=kCustom, calls=%fused_computation | custom fusion | bytes 8421376 | tf_op jit(solution)/shard_map/jit(_take)/gather | solution.py:22
  48.2 7.6 %select_select_fusion = bf16[64,128,256]{2,1,0:T(8,128)(2,1)} fusion(bf16[64,128,256]{2,1,0:T(8,128)(2,1)} %bitcast.47, pred[64,128]{1,0:T(8,128)(4,1)S(1)} %compare_and_fusion, pred[64,128]{1,0:T(8,128)(4,1)S(1)} %compare_bitcast_fusion), kind=kLoop, calls=%fused_computation.12 | loop fusion | flops 4194304 | bytes 8404992 | tf_op jit(solution)/shard_map/jit(_where)/select_n | solution.py:23
  55.8 12.4 %all-to-all-start = ((bf16[64,128,256]{2,1,0:T(8,128)(2,1)}), bf16[64,128,256]{2,1,0:T(8,128)(2,1)}, u32[]{:S(2)}, u32[]{:S(2)}) async-start(bf16[64,128,256]{2,1,0:T(8,128)(2,1)} %select_select_fusion), calls=%async_computation | async-start | bytes 8388608 | tf_op jit(solution)/shard_map/all_to_all | solution.py:24
  69.5 51.7 %all-to-all-done = bf16[64,128,256]{2,1,0:T(8,128)(2,1)} async-done(((bf16[64,128,256]{2,1,0:T(8,128)(2,1)}), bf16[64,128,256]{2,1,0:T(8,128)(2,1)}, u32[]{:S(2)}, u32[]{:S(2)}) %all-to-all-start) | async-done | bytes 4194336 | tf_op jit(solution)/shard_map/all_to_all | solution.py:24
  121.2 6.7 %copy.16 = bf16[8,8,128,256]{3,1,2,0:T(8,128)(2,1)} copy(bf16[8,8,128,256]{3,2,1,0:T(8,128)(2,1)} %bitcast.14) | data formatting | bytes 8388608
  128.0 45.7 %while.11 = (s32[]{:T(128)}, f32[16,32768]{1,0:T(8,128)S(1)}, s32[]{:T(128)}, s32[512]{0:T(512)S(1)}, bf16[512,128,128]{2,1,0:T(8,128)(2,1)}, /*index=5*/s32[512...) while((s32[]{:T(128)}, f32[16,32768]{1,0:T(8,128)S(1)}, ...), condition=%wide.region_2.3_spmd.clone, body=%wide.region_1.2_spmd.clone.sunk | while | flops 605555200 | bytes 34603944 | solution.py:57
  129.0 2.9 convolution_convert_fusion.3
  132.5 1.9 fusion.28
  134.4 2.4 copy.20
  136.9 2.7 convolution_add_fusion.2
  140.4 2.9 convolution_convert_fusion.3
  143.9 1.9 fusion.28
  145.8 2.4 copy.20
  148.2 2.7 convolution_add_fusion.2
  151.8 2.9 convolution_convert_fusion.3
  155.2 1.9 fusion.28
  157.2 2.4 copy.20
  159.6 2.7 convolution_add_fusion.2
  163.2 2.9 convolution_convert_fusion.3
  166.6 1.9 fusion.28
  168.5 2.4 copy.20
  171.0 2.7 convolution_add_fusion.2
  173.7 1.5 reshape.74
  175.2 148.7 %all-reduce.4 = bf16[2048,256]{1,0:T(8,128)(2,1)S(1)} all-reduce(f32[2048,256]{1,0:T(8,128)} %reshape.74), channel_id=1, replica_groups=mesh['row'=64,'rep'=2] {'rep'}, use_global_device_ids=true, to_apply=%region_3.4 | all-reduce | flops 524288 | bytes 3145728 | tf_op jit(solution)/shard_map/psum | solution.py:59
  324.0 1.2 convolution_bitcast_fusion
  325.2 1.4 convolution_convert_fusion.1
  326.6 117.7 %all-reduce.3.cloned.1.call-done = f32[256,256]{0,1:T(8,128)} async-done(((f32[256,256]{0,1:T(8,128)}), f32[256,256]{0,1:T(8,128)}) %all-reduce.3.cloned.1.call-update) | async-done | bytes 262160 | tf_op jit(solution)/shard_map/psum | solution.py:66
  444.3 1.0 broadcast_multiply_fusion
  (29 shorter events, 8.6 us)
Async XLA Ops:
  7.2 316.8 %copy-start = (bf16[2048,256]{1,0:T(8,128)(2,1)S(1)}, bf16[2048,256]{1,0:T(8,128)(2,1)}, u32[]{:S(2)}) copy-start(bf16[2048,256]{1,0:T(8,128)(2,1)} %param.10) | copy-start | bytes 3145732
  55.8 12.4 %copy-start.2 = (s32[1,1,512]{2,1,0:T(1,128)S(1)}, s32[1,1,512]{2,1,0:T(1,128)}, u32[]{:S(2)}) copy-start(s32[1,1,512]{2,1,0:T(1,128)} %param.16) | copy-start | bytes 6148
  55.8 65.4 %all-to-all-start = ((bf16[64,128,256]{2,1,0:T(8,128)(2,1)}), bf16[64,128,256]{2,1,0:T(8,128)(2,1)}, u32[]{:S(2)}, u32[]{:S(2)}) async-start(bf16[64,128,256]{2,1,0:T(8,128)(2,1)} %select_select_fusion), calls=%async_computation | async-start | bytes 8388608 | tf_op jit(solution)/shard_map/all_to_all | solution.py:24
  68.2 376.1 %all-reduce.3.cloned.1.call-start = ((), (), s32[]{:S(2)}) async-start(), calls=%async_computation.1 | async-start | bytes 524288 | tf_op jit(solution)/shard_map/psum | solution.py:66
  173.7 151.5 %copy-start.1 = (bf16[256,256]{1,0:T(8,128)(2,1)S(1)}, bf16[256,256]{1,0:T(8,128)(2,1)}, u32[]{:S(2)}) copy-start(bf16[256,256]{1,0:T(8,128)(2,1)} %param.13) | copy-start | bytes 393220
Sparse Core Ops, SparseCore 0:
  325.3 118.9 all-reduce.2
where the time goes:
time: 456 us; the launch traced here: 453 us
  waiting for transfers between devices  169 us (37%)
  blocking collectives  149 us (33%)
  local copies, waits for them, and re-layouts  60.4 us (13%)
  matrix products  32.9 us (7%)
  between operations  14.8 us (3%)
  other arithmetic  14 us (3%)
  starting transfers between devices  12.4 us (3%)
    psum x1, blocking collectives, local(): agg = lax.psum(partial_value, 'rep').astype(jnp.bfloat16)  149 us
    psum x1, waiting for transfers between devices, local(): w_sum = lax.psum(w_term, 'row')  118 us
    all_to_all x1, waiting for transfers between devices, local(): lax.all_to_all(picked, 'row', split_axis=0, concat_axis=0, tiled=True)  51.7 us
    gather x1, local copies, waits for them, and re-layouts, local(): jnp.take(grad_pre, safe.reshape(-1), axis=0)  33.1 us
    all_to_all x1, starting transfers between devices, local(): lax.all_to_all(picked, 'row', split_axis=0, concat_axis=0, tiled=True)  12.4 us
    dot_general x4, matrix products, add_block(): jnp.dot(peer_hot, flat_received, preferred_element_type=jnp.float32)  11.8 us
    while x8, local copies, waits for them, and re-layouts  11.7 us
    dot_general x4, matrix products, add_block(): jnp.dot(row_hot, prods.reshape(block, tile * width), precision=lax.Precis...  10.7 us
  transfers between devices with their start and end apart: 2, of which 2 were waited for; matrix products, arithmetic and copies ran while one was open for 0% of the time, Pallas kernels for 0%

commit v1 on v0

--- a/solution.py
+++ b/solution.py
@@ -1,27 +1,210 @@
+import functools
 import math
 
 import jax
 import jax.numpy as jnp
 from jax import lax
+from jax.experimental import pallas as pl
+from jax.experimental.pallas import tpu as pltpu
 from jax.sharding import PartitionSpec as P
 
-
-def unpack_mask(mask_bits):
-    shifts = jnp.arange(16, dtype=jnp.int32)
-    bits = jnp.bitwise_and(jnp.right_shift(mask_bits[:, :, None], shifts[None, None, :]), 1)
-    return bits.reshape(mask_bits.shape[0], mask_bits.shape[1] * 16)
+MESH = pl.DeviceIdType.MESH
+SIDE = 4
+UORDER = (0, 7, 1, 6, 2, 5, 3, 4)
+
+
+def place(me):
+    return me % SIDE, me // (SIDE * SIDE), (me // SIDE) % SIDE
+
+
+def shifted(me, off, sign):
+    x, y, z = place(me)
+    dx, dy, dz = off
+    return (
+        ((y + sign * dy + SIDE) % SIDE) * SIDE + (z + sign * dz + SIDE) % SIDE
+    ) * SIDE + (x + sign * dx + SIDE) % SIDE
+
+
+def offset_of(i, u):
+    g, w = 7 - i, UORDER[u]
+    return (
+        g % 2 + 2 * (w & 1),
+        (g // 2) % 2 + 2 * ((w >> 1) & 1),
+        g // 4 + 2 * (w >> 2),
+    )
+
+
+def front_kernel(
+    og_ref, mb_ref, sr_ref, recv_ref,
+    gp, listed, turned, wide, hot, sbuf,
+    ssem, rsem, fssem, frsem, own_sem,
+):
+    me = lax.axis_index("row")
+    core = lax.axis_index("rep")
+    rows, width = gp.shape
+    half = sbuf.shape[1]
+    tile = 2 * half
+
+    barrier = pltpu.get_barrier_semaphore()
+    pl.semaphore_signal(barrier, inc=1, device_id=(me, 1 - core), device_id_type=MESH)
+
+    @pl.loop(1, 64)
+    def _(j):
+        q = shifted(me, (j % 4, (j // 4) % 4, j // 16), 1)
+        pl.semaphore_signal(barrier, inc=1, device_id=(q, core), device_id_type=MESH)
+
+    words = mb_ref.shape[1]
+    feature = lax.broadcasted_iota(jnp.int32, (words, width), 1)
+    word = lax.broadcasted_iota(jnp.int32, (words, width), 0)
+    here = feature // 16 == word
+    low = jnp.where(here & (feature % 16 < 8), 1.0, 0.0).astype(jnp.bfloat16)
+    high = jnp.where(here & (feature % 16 >= 8), 1.0, 0.0).astype(jnp.bfloat16)
+    step = 256
+    bit = lax.broadcasted_iota(jnp.int32, (step, width), 1) % 8
+
+    @pl.loop(0, rows // step)
+    def _(b):
+        at = pl.ds(pl.multiple_of(b * step, step), step)
+        bits = mb_ref[at, :]
+        lo = (bits & 255).astype(jnp.float32).astype(jnp.bfloat16)
+        hi = (bits >> 8).astype(jnp.float32).astype(jnp.bfloat16)
+        byte = jnp.dot(lo, low, preferred_element_type=jnp.float32)
+        byte += jnp.dot(hi, high, preferred_element_type=jnp.float32)
+        keep = (byte.astype(jnp.int32) >> bit) & 1
+        grad = og_ref[at, :].astype(jnp.float32)
+        gp[at, :] = jnp.where(keep == 1, grad, 0.0).astype(jnp.bfloat16)
+
+    listed[...] = jnp.full(listed.shape, -1, jnp.int32)
+    for u in range(8):
+
+        @pl.loop(0, 8)
+        def _(i, u=u):
+            q = shifted(me, offset_of(i, u), 1)
+            listed[pl.ds(i * 8 + u, 1), :] = sr_ref[pl.ds(q, 1), :]
+
+    turned[...] = listed[...].T
+    mine = turned[pl.ds(pl.multiple_of(core * half, half), half), :]
+    for j in range(64):
+        wide[j] = jnp.broadcast_to(mine[:, j : j + 1], (half, 128))
+
+    lane = lax.broadcasted_iota(jnp.int32, (half, 128), 1)
+    halves = pl.ds(pl.multiple_of(core * half, half), half)
+
+    def send(i, u):
+        q = shifted(me, offset_of(i, u), 1)
+        j = i * 8 + u
+        return pltpu.make_async_remote_copy(
+            src_ref=sbuf.at[j], dst_ref=recv_ref.at[me, halves],
+            send_sem=ssem.at[j], recv_sem=rsem.at[j],
+            device_id=(q, core), device_id_type=MESH,
+        )
+
+    def forward(i, u):
+        p = shifted(me, offset_of(i, u), -1)
+        j = i * 8 + u
+        return pltpu.make_async_remote_copy(
+            src_ref=recv_ref.at[p, halves], dst_ref=recv_ref.at[p, halves],
+            send_sem=fssem.at[j], recv_sem=frsem.at[j],
+            device_id=(me, 1 - core), device_id_type=MESH,
+        )
+
+    def keep_own():
+        return pltpu.make_async_copy(sbuf.at[56], recv_ref.at[me, halves], own_sem)
+
+    @pl.loop(0, 8)
+    def _(i):
+        for u in range(8):
+            listed_at = wide[i * 8 + u]
+            block = listed_at >> 7
+            one = jnp.where((listed_at & 127) == lane, 1.0, 0.0)
+            for t in range(rows // 128):
+                hot[u * half : (u + 1) * half, t * 128 : (t + 1) * 128] = jnp.where(
+                    block == t, one, 0.0
+                ).astype(jnp.bfloat16)
+        picked = jnp.dot(hot[...], gp[...], preferred_element_type=jnp.float32)
+        for u in range(8):
+            sbuf[i * 8 + u] = picked[u * half : (u + 1) * half].astype(jnp.bfloat16)
+
+        @pl.when(i == 0)
+        def _():
+            pl.semaphore_wait(barrier, 64)
+
+        for u in range(8):
+            if u == 0:
+
+                @pl.when(i < 7)
+                def _(u=u):
+                    send(i, u).start()
+
+                @pl.when(i == 7)
+                def _():
+                    keep_own().start()
+            else:
+                send(i, u).start()
+
+    @pl.loop(0, 8)
+    def _(i):
+        for u in range(8):
+            if u == 0:
+
+                @pl.when(i < 7)
+                def _(u=u):
+                    send(i, u).wait_recv()
+
+                @pl.when(i == 7)
+                def _():
+                    keep_own().wait()
+            else:
+                send(i, u).wait_recv()
+            forward(i, u).start()
+
+    @pl.loop(0, 8)
+    def _(i):
+        for u in range(8):
+            if u == 0:
+
+                @pl.when(i < 7)
+                def _(u=u):
+                    send(i, u).wait_send()
+            else:
+                send(i, u).wait_send()
+            forward(i, u).wait()
+
+
+def front(out_grad, mask_bits, listed):
+    rows, width = out_grad.shape
+    peers, tile = listed.shape
+    half = tile // 2
+    vmem = pl.BlockSpec(memory_space=pltpu.VMEM)
+    return pl.pallas_call(
+        front_kernel,
+        out_shape=jax.ShapeDtypeStruct((peers, tile, width), jnp.bfloat16),
+        in_specs=[vmem, vmem, vmem],
+        out_specs=pl.BlockSpec(memory_space=pl.ANY),
+        scratch_shapes=[
+            pltpu.VMEM((rows, width), jnp.bfloat16),
+            pltpu.VMEM((128, 128), jnp.int32),
+            pltpu.VMEM((128, 128), jnp.int32),
+            pltpu.VMEM((peers, half, 128), jnp.int32),
+            pltpu.VMEM((8 * half, rows), jnp.bfloat16),
+            pltpu.VMEM((peers, half, width), jnp.bfloat16),
+            pltpu.SemaphoreType.DMA((peers,)),
+            pltpu.SemaphoreType.DMA((peers,)),
+            pltpu.SemaphoreType.DMA((peers,)),
+            pltpu.SemaphoreType.DMA((peers,)),
+            pltpu.SemaphoreType.DMA,
+        ],
+        compiler_params=pltpu.CompilerParams(
+            collective_id=0, has_side_effects=True, vmem_limit_bytes=32 * 2**20
+        ),
+        name="front",
+    )(out_grad, mask_bits, listed)
 
 
 def local(node_feats, out_grad, mask_bits, weight, send_rows, tile_vals, tile_row, tile_peer):
     rows_here = node_feats.shape[0]
     width = node_feats.shape[1]
-    mask = unpack_mask(mask_bits)
-    grad_pre = jnp.where(mask == 1, out_grad, jnp.zeros_like(out_grad))
-    listed = send_rows[0]
-    safe = jnp.clip(listed, 0, rows_here - 1)
-    picked = jnp.take(grad_pre, safe.reshape(-1), axis=0).reshape(listed.shape + (width,))
-    picked = jnp.where(listed[:, :, None] >= 0, picked, jnp.zeros_like(picked))
-    received = lax.all_to_all(picked, "row", split_axis=0, concat_axis=0, tiled=True)
+    received = front(out_grad, mask_bits, send_rows[0])
     values = tile_vals[0, 0]
     rows = tile_row[0, 0]
     peers = tile_peer[0, 0]

time: 456 us -> 398 us (0.87)
  waiting for transfers between devices: 169 us -> 119 us
  blocking collectives: 149 us -> 106 us
  Pallas kernels: 0 us -> 42.9 us
  matrix products: 32.9 us -> 63.1 us
  local copies, waits for them, and re-layouts: 60.4 us -> 45.7 us
  starting transfers between devices: 12.4 us -> 0.04 us
  other arithmetic: 14 us -> 2.37 us
    all_to_all x1 -> x0, waiting for transfers between devices: 51.7 us -> none  [local(): lax.all_to_all(picked, 'row', split_axis=0, concat_axis=0, tiled=True)]
    pallas_call x0 -> x1, Pallas kernels: none -> 42.9 us  [front(): pl.pallas_call(front_kernel, out_shape=jax.ShapeDtypeStruct((peers, tile,...]
    psum x1, blocking collectives: 149 us -> 106 us  [local(): agg = lax.psum(partial_value, 'rep').astype(jnp.bfloat16)]
    gather x1 -> x0, local copies, waits for them, and re-layouts: 33.1 us -> none  [local(): jnp.take(grad_pre, safe.reshape(-1), axis=0)]
    all_to_all x1 -> x0, starting transfers between devices: 12.4 us -> none  [local(): lax.all_to_all(picked, 'row', split_axis=0, concat_axis=0, tiled=True)]
    dot_general x4 -> x8, matrix products: 11.8 us -> 23.5 us  [add_block(): jnp.dot(peer_hot, flat_received, preferred_element_type=jnp.float32)]
    while x8 -> x16, local copies, waits for them, and re-layouts: 11.7 us -> 23.4 us
    dot_general x4 -> x8, matrix products: 10.7 us -> 21.5 us  [add_block(): jnp.dot(row_hot, prods.reshape(block, tile * width), precision=lax.Precis...]
  transfers between devices with their start and end apart: 2 -> 1, of which waited for: 2 -> 1; matrix products, arithmetic and copies ran while one was open for 0% -> 0% of each run, Pallas kernels for 0% -> 0%
where the time goes in v1:
time: 398 us; the launch traced here: 395 us
  waiting for transfers between devices  119 us (30%)
  blocking collectives  106 us (27%)
  matrix products  63.1 us (16%)
  local copies, waits for them, and re-layouts  45.7 us (11%)
  Pallas kernels  42.9 us (11%)
  between operations  14.8 us (4%)
    psum x1, waiting for transfers between devices, local(): w_sum = lax.psum(w_term, 'row')  119 us
    psum x1, blocking collectives, local(): agg = lax.psum(partial_value, 'rep').astype(jnp.bfloat16)  106 us
    pallas_call x1, Pallas kernels, front(): pl.pallas_call(front_kernel, out_shape=jax.ShapeDtypeStruct((peers, tile,...  42.9 us
    dot_general x8, matrix products, add_block(): jnp.dot(peer_hot, flat_received, preferred_element_type=jnp.float32)  23.5 us
    while x16, local copies, waits for them, and re-layouts  23.4 us
    dot_general x8, matrix products, add_block(): jnp.dot(row_hot, prods.reshape(block, tile * width), precision=lax.Precis...  21.5 us
    dot_general x8, matrix products, add_block(): jnp.einsum('kab,kbf->kaf', block_vals, sources, preferred_element_type=jn...  15.4 us
    unnamed x11, local copies, waits for them, and re-layouts  8.6 us
  transfers between devices with their start and end apart: 1, of which 1 were waited for; matrix products, arithmetic and copies ran while one was open for 0% of the time, Pallas kernels for 0%

profile of v1, /device:TPU:1, one launch (start us, length us, event | category | flops | bytes accessed | tf_op | source)
XLA Modules:
  0.0 394.9 jit_solution(16694066104701415892)
XLA Ops:
  12.5 42.9 %front.1 = bf16[64,128,256]{2,1,0:T(8,128)(2,1)S(1)} custom-call(bf16[2048,256]{1,0:T(8,128)(2,1)S(1)} %copy-done.1, s32[2048,16]{1,0:T(8,128)S(1)} %copy.10.mb_ref, s32[64,128]{1,0:T(8,128)S(1)} %bitcast.34), custom_call_target="tpu_custom_call" | custom-call | tf_op jit(solution)/shard_map/front/pallas_call | solution.py:179
  55.5 4.5 %copy.14 = bf16[8,8,128,256]{3,1,2,0:T(8,128)(2,1)} copy(bf16[8,8,128,256]{3,2,1,0:T(8,128)(2,1)S(1)} %bitcast.33) | data formatting | bytes 8388608
  60.1 96.5 %while.11 = (s32[]{:T(128)}, f32[16,32768]{1,0:T(8,128)S(1)}, s32[]{:T(128)}, s32[512]{0:T(512)}, bf16[512,128,128]{2,1,0:T(8,128)(2,1)}, /*index=5*/s32[512]{0:...) while((s32[]{:T(128)}, f32[16,32768]{1,0:T(8,128)S(1)}, ...), condition=%wide.region_2.3_spmd.clone, body=%wide.region_1.2_spmd.clone.sunk | while | flops 605555200 | bytes 34603944 | solution.py:240
  61.9 2.9 convolution_convert_fusion.3
  65.3 1.9 fusion.27
  67.2 2.4 copy.18
  69.7 2.7 convolution_add_fusion.2
  73.9 2.9 convolution_convert_fusion.3
  79.3 2.4 copy.18
  81.7 2.7 convolution_add_fusion.2
  85.9 2.9 convolution_convert_fusion.3
  89.4 1.9 fusion.27
  91.3 2.4 copy.18
  93.8 2.7 convolution_add_fusion.2
  98.0 2.9 convolution_convert_fusion.3
  101.4 1.9 fusion.27
  103.4 2.4 copy.18
  105.8 2.7 convolution_add_fusion.2
  110.0 2.9 convolution_convert_fusion.3
  115.4 2.4 copy.18
  117.8 2.7 convolution_add_fusion.2
  122.1 2.9 convolution_convert_fusion.3
  127.4 2.4 copy.18
  129.9 2.7 convolution_add_fusion.2
  134.1 2.9 convolution_convert_fusion.3
  139.5 2.4 copy.18
  141.9 2.7 convolution_add_fusion.2
  146.2 2.9 convolution_convert_fusion.3
  151.5 2.4 copy.18
  154.0 2.7 convolution_add_fusion.2
  158.2 106.0 %all-reduce.4 = bf16[2048,256]{1,0:T(8,128)(2,1)S(1)} all-reduce(f32[2048,256]{1,0:T(8,128)} %reshape.21), channel_id=1, replica_groups=mesh['row'=64,'rep'=2] {'rep'}, use_global_device_ids=true, to_apply=%region_3.4 | all-reduce | flops 524288 | bytes 3145728 | tf_op jit(solution)/shard_map/psum | solution.py:242
  266.8 119.4 %all-reduce.3.cloned.1.call-done = f32[256,256]{0,1:T(8,128)} async-done(((f32[256,256]{0,1:T(8,128)}), f32[256,256]{0,1:T(8,128)}) %all-reduce.3.cloned.1.call-update) | async-done | bytes 262160 | tf_op jit(solution)/shard_map/psum | solution.py:249
  (47 shorter events, 36.4 us)
Async XLA Ops:
  7.2 257.0 %copy-start = (bf16[2048,256]{1,0:T(8,128)(2,1)S(1)}, bf16[2048,256]{1,0:T(8,128)(2,1)}, u32[]{:S(2)}) copy-start(bf16[2048,256]{1,0:T(8,128)(2,1)} %param.10) | copy-start | bytes 3145732
  7.2 379.0 %all-reduce.3.cloned.1.call-start = ((), (), s32[]{:S(2)}) async-start(), calls=%async_computation | async-start | bytes 524288 | tf_op jit(solution)/shard_map/psum | solution.py:249
  10.5 1.2 copy-start.1
  11.8 0.8 copy-start.2
  264.2 1.2 copy-start.3
Sparse Core Ops, SparseCore 0:
  265.5 120.6 all-reduce.2

commit v2 on v1

v2 whole, which is shorter than its diff:
```python
import math

import jax
import jax.numpy as jnp
from jax import lax
from jax.experimental import pallas as pl
from jax.experimental.pallas import tpu as pltpu
from jax.sharding import PartitionSpec as P

MESH = pl.DeviceIdType.MESH
SIDE = 4
UORDER = (0, 7, 1, 6, 2, 5, 3, 4)
GROUP = 4
UNROLL = 20
PLANE = [(0, a, b) for a in range(4) for b in range(4) if (a, b) != (0, 0)]
LINE = [(a, 0, 0) for a in range(1, 4)]


def place(me):
    return me % SIDE, me // (SIDE * SIDE), (me // SIDE) % SIDE


def shifted(me, off, sign):
    x, y, z = place(me)
    dx, dy, dz = off
    return (
        ((y + sign * dy + SIDE) % SIDE) * SIDE + (z + sign * dz + SIDE) % SIDE
    ) * SIDE + (x + sign * dx + SIDE) % SIDE


def offset_of(i, u):
    g, w = 7 - i, UORDER[u]
    return (
        g % 2 + 2 * (w & 1),
        (g // 2) % 2 + 2 * ((w >> 1) & 1),
        g // 4 + 2 * (w >> 2),
    )


def iota(shape, dim):
    return lax.broadcasted_iota(jnp.int32, shape, dim)


def layout_tables(row, peer, row_tiles, zero_peer, places):
    slots = row.shape[1]
    key = jnp.where(row < 0, row_tiles, row)
    key_down = jnp.broadcast_to(key, (128, slots)).T
    peer_down = jnp.broadcast_to(peer, (128, slots)).T
    down = iota((slots, 128), 0)
    across = iota((slots, 128), 1)
    count = jnp.sum((key_down == across).astype(jnp.int32), axis=0, keepdims=True)
    groups = jnp.where(iota((1, 128), 1) < row_tiles, (count + GROUP - 1) // GROUP, 0)
    groups_down = jnp.broadcast_to(groups, (128, 128)).T
    r_down, r_across = iota((128, 128), 0), iota((128, 128), 1)
    first = jnp.sum(jnp.where(r_down < r_across, groups_down, 0), axis=0, keepdims=True)
    first_down = jnp.broadcast_to(first, (128, 128)).T

    spots = []
    for b in range(slots // 128):
        key_here = key[:, b * 128 : (b + 1) * 128]
        before = (key_down == key_here) & (down < across + b * 128)
        rank = jnp.sum(before.astype(jnp.int32), axis=0, keepdims=True)
        base = jnp.sum(jnp.where(r_down < key_here, groups_down, 0), axis=0, keepdims=True)
        spots.append(jnp.where(key_here < row_tiles, base * GROUP + rank, -1))
    spot_down = jnp.broadcast_to(jnp.concatenate(spots, axis=1), (128, slots)).T

    slot_at, peer_at, goes_on = [], [], []
    for b in range(places // 128):
        hit = spot_down == across + b * 128
        slot_at.append(jnp.sum(jnp.where(hit, down, 0), axis=0, keepdims=True))
        peer_at.append(
            jnp.sum(jnp.where(hit, peer_down - zero_peer, 0), axis=0, keepdims=True) + zero_peer
        )
        opens = (first_down == r_across + b * 128) & (groups_down > 0)
        goes_on.append(1 - jnp.sum(opens.astype(jnp.int32), axis=0, keepdims=True))
    last = jnp.where(groups > 0, first + groups, 0)
    last = jnp.concatenate([last, jnp.zeros((1, places - 128), jnp.int32)], axis=1)
    rows = [jnp.concatenate(part, axis=1) for part in (slot_at, peer_at, goes_on)] + [last]
    return jnp.concatenate(rows + [jnp.zeros((8 - len(rows), places), jnp.int32)], axis=0)


def kernel(
    scale,
    og_hbm, mb_hbm, sr_hbm, row_hbm, peer_hbm, nf_hbm, wt_hbm, tv_hbm,
    ing_hbm, wg_hbm,
    og, mb, sr, row_v, peer_v, nf, wt, tv,
    gp, listed, turned, wide, hot, sbuf, recv, table_v, table_s,
    steps, part, other, nft, ing, agg, term, red, line, done,
    in_sem, tv_sem, table_sem, own_sem, out_sem,
    ssem, rsem, fssem, frsem, pssem, prsem, r1s, r1r, r2s, r2r, r3s, r3r,
):
    me = lax.axis_index("row")
    core = lax.axis_index("rep")
    rows, width = gp.shape
    peers, half = sbuf.shape[:2]
    tile = 2 * half
    row_tiles = rows // tile
    sib = (me, 1 - core)

    loads = [
        pltpu.make_async_copy(src, dst, in_sem.at[n])
        for n, (src, dst) in enumerate(
            (
                (sr_hbm, sr), (mb_hbm, mb), (og_hbm, og), (row_hbm, row_v),
                (peer_hbm, peer_v), (nf_hbm, nf), (wt_hbm, wt),
            )
        )
    ]
    for load in loads[:5]:
        load.start()

    barrier = pltpu.get_barrier_semaphore()
    pl.semaphore_signal(barrier, inc=1, device_id=sib, device_id_type=MESH)

    @pl.loop(1, 64)
    def _(j):
        q = shifted(me, (j % 4, (j // 4) % 4, j // 16), 1)
        pl.semaphore_signal(barrier, inc=1, device_id=(q, core), device_id_type=MESH)

    for off in PLANE:
        q = shifted(me, off, 1)
        pl.semaphore_signal(barrier, inc=1, device_id=(q, 1 - core), device_id_type=MESH)
    greeted = 1 + 63 + len(PLANE)

    loads[0].wait()
    listed[...] = jnp.full(listed.shape, -1, jnp.int32)
    for u in range(8):

        @pl.loop(0, 8)
        def _(i, u=u):
            q = shifted(me, offset_of(i, u), 1)
            listed[pl.ds(i * 8 + u, 1), :] = sr[pl.ds(q, 1), :]

    turned[...] = listed[...].T
    mine = turned[pl.ds(pl.multiple_of(core * half, half), half), :]
    for j in range(64):
        wide[j] = jnp.broadcast_to(mine[:, j : j + 1], (half, 128))

    words = mb.shape[0]
    feature = iota((2 * words, width), 1)
    byte_at = iota((2 * words, width), 0)
    spread = (feature // 16 == byte_at % words) & ((feature % 16 >= 8) == (byte_at >= words))
    spread = jnp.where(spread, 1.0, 0.0).astype(jnp.bfloat16)
    step = 256
    bit = iota((step, width), 1) % 8
    loads[1].wait()
    loads[2].wait()

    @pl.loop(0, rows // step)
    def _(b):
        at = pl.ds(pl.multiple_of(b * step, step), step)
        bits = mb[:, at]
        both = jnp.concatenate([bits & 255, bits >> 8], axis=0)
        both = both.astype(jnp.float32).astype(jnp.bfloat16)
        byte = lax.dot_general(
            both, spread, (((0,), (0,)), ((), ())), preferred_element_type=jnp.float32
        )
        keep = (byte.astype(jnp.int32) >> bit) & 1
        grad = og[at, :].astype(jnp.float32)
        gp[at, :] = jnp.where(keep == 1, grad, 0.0).astype(jnp.bfloat16)

    lane = iota((half, 128), 1)
    halves = pl.ds(pl.multiple_of(core * half, half), half)

    def send(i, u):
        q = shifted(me, offset_of(i, u), 1)
        j = i * 8 + u
        return pltpu.make_async_remote_copy(
            src_ref=sbuf.at[j], dst_ref=recv.at[me, halves],
            send_sem=ssem.at[j], recv_sem=rsem.at[j],
            device_id=(q, core), device_id_type=MESH,
        )

    def forward(i, u):
        p = shifted(me, offset_of(i, u), -1)
        j = i * 8 + u
        return pltpu.make_async_remote_copy(
            src_ref=recv.at[p, halves], dst_ref=recv.at[p, halves],
            send_sem=fssem.at[j], recv_sem=frsem.at[j],
            device_id=sib, device_id_type=MESH,
        )

    def keep_own():
        return pltpu.make_async_copy(sbuf.at[peers - 8], recv.at[me, halves], own_sem)

    @pl.loop(0, 8)
    def _(i):
        for u in range(8):
            listed_at = wide[i * 8 + u]
            block = listed_at >> 7
            one = jnp.where((listed_at & 127) == lane, 1.0, 0.0)
            for t in range(rows // 128):
                hot[u * half : (u + 1) * half, t * 128 : (t + 1) * 128] = jnp.where(
                    block == t, one, 0.0
                ).astype(jnp.bfloat16)
        picked = jnp.dot(hot[...], gp[...], preferred_element_type=jnp.float32)
        for u in range(8):
            sbuf[i * 8 + u] = picked[u * half : (u + 1) * half].astype(jnp.bfloat16)

        @pl.when(i == 0)
        def _():
            pl.semaphore_wait(barrier, greeted)

        for u in range(8):
            if u == 0:

                @pl.when(i < 7)
                def _(u=u):
                    send(i, u).start()

                @pl.when(i == 7)
                def _():
                    keep_own().start()
            else:
                send(i, u).start()

    fill = pltpu.make_async_copy(tv_hbm, tv, tv_sem)
    fill.start()
    for load in loads[5:]:
        load.start()
    loads[3].wait()
    loads[4].wait()
    table_v[...] = layout_tables(
        row_v[...], peer_v[...], row_tiles, peers, table_v.shape[1]
    )
    table_copy = pltpu.make_async_copy(table_v, table_s, table_sem)
    table_copy.start()
    recv[peers] = jnp.zeros(recv.shape[1:], recv.dtype)
    steps[0] = jnp.zeros(steps.shape[1:], steps.dtype)
    loads[5].wait()
    loads[6].wait()
    columns = pl.ds(pl.multiple_of(core * 128, 128), 128)

    @pl.loop(0, row_tiles)
    def _(r):
        at = pl.ds(pl.multiple_of(r * tile, tile), tile)
        nft[r] = nf[at, columns].T

    table_copy.wait()

    @pl.loop(0, 8)
    def _(i):
        for u in range(8):
            if u == 0:

                @pl.when(i < 7)
                def _(u=u):
                    send(i, u).wait_recv()

                @pl.when(i == 7)
                def _():
                    keep_own().wait()
            else:
                send(i, u).wait_recv()
            forward(i, u).start()

    @pl.loop(0, 8)
    def _(i):
        for u in range(8):
            if u == 0:

                @pl.when(i < 7)
                def _(u=u):
                    send(i, u).wait_send()
            else:
                send(i, u).wait_send()
            forward(i, u).wait()

    fill.wait()

    @pl.loop(0, (steps.shape[0] - 1) // UNROLL)
    def _(i):
        for u in range(UNROLL):
            g = i * UNROLL + u
            left = jnp.concatenate([tv[table_s[0, GROUP * g + v]] for v in range(GROUP)], axis=1)
            right = jnp.concatenate([recv[table_s[1, GROUP * g + v]] for v in range(GROUP)], axis=0)
            prod = jnp.dot(left, right, preferred_element_type=jnp.float32)
            steps[g + 1] = jnp.where(table_s[2, g] == 1, steps[g], 0.0) + prod

    def swap(r):
        return pltpu.make_async_remote_copy(
            src_ref=part.at[r], dst_ref=other.at[r],
            send_sem=pssem.at[r], recv_sem=prsem.at[r],
            device_id=sib, device_id_type=MESH,
        )

    for r in range(row_tiles):
        part[r] = steps[table_s[3, r]]
        swap(r).start()
    term[...] = jnp.zeros(term.shape, term.dtype)
    for b in range(row_tiles // GROUP):
        for r in range(b * GROUP, (b + 1) * GROUP):
            swap(r).wait()
            agg[r * tile : (r + 1) * tile, :] = (part[r] + other[r]).astype(jnp.bfloat16)
        at = slice(b * GROUP * tile, (b + 1) * GROUP * tile)
        left = jnp.concatenate([nft[b * GROUP + v] for v in range(GROUP)], axis=1)
        term[...] += jnp.dot(left, agg[at, :], preferred_element_type=jnp.float32)

    x, y, z = place(me)
    spot = y * SIDE + z
    piece = red.shape[1]

    def rows_of(s):
        return pl.ds(pl.multiple_of(s * piece, piece), piece)

    def first_send(n):
        q = shifted(me, PLANE[n], 1)
        return pltpu.make_async_remote_copy(
            src_ref=term.at[rows_of(q // SIDE)], dst_ref=red.at[n],
            send_sem=r1s.at[n], recv_sem=r1r.at[n],
            device_id=(q, core), device_id_type=MESH,
        )

    def second_send(n):
        return pltpu.make_async_remote_copy(
            src_ref=line.at[x], dst_ref=line.at[x],
            send_sem=r2s.at[n], recv_sem=r2r.at[n],
            device_id=(shifted(me, LINE[n], 1), core), device_id_type=MESH,
        )

    def third_send(n):
        if n < 2 * len(PLANE):
            to = (shifted(me, PLANE[n // 2], 1), core if n % 2 == 0 else 1 - core)
        else:
            to = sib
        at = pl.ds(pl.multiple_of(core * 128 + spot * piece, piece), piece)
        return pltpu.make_async_remote_copy(
            src_ref=done.at[at], dst_ref=done.at[at],
            send_sem=r3s.at[n], recv_sem=r3r.at[n],
            device_id=to, device_id_type=MESH,
        )

    for n in range(len(PLANE)):
        first_send(n).start()

    @pl.loop(0, rows // 512)
    def _(b):
        at = pl.ds(pl.multiple_of(b * 512, 512), 512)
        ing[at, :] = lax.dot_general(
            agg[at, :], wt[...], (((1,), (1,)), ((), ())), preferred_element_type=jnp.float32
        ).astype(jnp.bfloat16)

    out_copy = pltpu.make_async_copy(ing, ing_hbm, out_sem.at[0])
    out_copy.start()
    mine_sum = term[rows_of(spot), :]
    for n in range(len(PLANE)):
        first_send(n).wait_recv()
        mine_sum += red[n]
    line[x] = mine_sum
    for n in range(len(LINE)):
        second_send(n).start()
    for n in range(len(LINE)):
        second_send(n).wait_recv()
    total = ((line[0] + line[1]) + line[2]) + line[3]
    done[pl.ds(pl.multiple_of(core * 128 + spot * piece, piece), piece), :] = total * jnp.float32(scale)
    thirds = 2 * len(PLANE) + 1
    for n in range(thirds):
        third_send(n).start()
    for n in range(thirds):
        third_send(n).wait_recv()
    w_copy = pltpu.make_async_copy(done, wg_hbm, out_sem.at[1])
    w_copy.start()
    for n in range(len(PLANE)):
        first_send(n).wait_send()
    for n in range(len(LINE)):
        second_send(n).wait_send()
    for n in range(thirds):
        third_send(n).wait_send()
    out_copy.wait()
    w_copy.wait()


def local(node_feats, out_grad, mask_bits, weight, send_rows, tile_vals, tile_row, tile_peer):
    rows, width = node_feats.shape
    peers, tile = send_rows.shape[1:]
    slots = tile_vals.shape[2]
    half = tile // 2
    row_tiles = rows // tile
    words = mask_bits.shape[1]
    most = -(-(slots + row_tiles * (GROUP - 1)) // GROUP)
    most = -(-most // UNROLL) * UNROLL
    places = -(-most * GROUP // 128) * 128
    piece = width // 2 // 16
    scale = 1.0 / math.sqrt(rows * lax.axis_size("row"))
    anywhere = pl.BlockSpec(memory_space=pl.ANY)
    bf16, f32, i32 = jnp.bfloat16, jnp.float32, jnp.int32
    dma = pltpu.SemaphoreType.DMA
    thirds = 2 * len(PLANE) + 1
    return pl.pallas_call(
        lambda *refs: kernel(scale, *refs),
        out_shape=(
            jax.ShapeDtypeStruct((rows, width), bf16),
            jax.ShapeDtypeStruct((width, width), f32),
        ),
        in_specs=[anywhere] * 8,
        out_specs=(anywhere, anywhere),
        scratch_shapes=[
            pltpu.VMEM((rows, width), bf16),
            pltpu.VMEM((words, rows), i32),
            pltpu.VMEM((peers, tile), i32),
            pltpu.VMEM((1, slots), i32),
            pltpu.VMEM((1, slots), i32),
            pltpu.VMEM((rows, width), bf16),
            pltpu.VMEM((width, width), bf16),
            pltpu.VMEM((slots, tile, tile), bf16),
            pltpu.VMEM((rows, width), bf16),
            pltpu.VMEM((128, 128), i32),
            pltpu.VMEM((128, 128), i32),
            pltpu.VMEM((peers, half, 128), i32),
            pltpu.VMEM((8 * half, rows), bf16),
            pltpu.VMEM((peers, half, width), bf16),
            pltpu.VMEM((peers + 1, tile, width), bf16),
            pltpu.VMEM((8, places), i32),
            pltpu.SMEM((8, places), i32),
            pltpu.VMEM((most + 1, tile, width), f32),
            pltpu.VMEM((row_tiles, tile, width), f32),
            pltpu.VMEM((row_tiles, tile, width), f32),
            pltpu.VMEM((row_tiles, width // 2, tile), bf16),
            pltpu.VMEM((rows, width), bf16),
            pltpu.VMEM((rows, width), bf16),
            pltpu.VMEM((width // 2, width), f32),
            pltpu.VMEM((len(PLANE), piece, width), f32),
            pltpu.VMEM((SIDE, piece, width), f32),
            pltpu.VMEM((width, width), f32),
            dma((7,)), dma, dma, dma, dma((2,)),
            dma((peers,)), dma((peers,)), dma((peers,)), dma((peers,)),
            dma((row_tiles,)), dma((row_tiles,)),
            dma((len(PLANE),)), dma((len(PLANE),)),
            dma((len(LINE),)), dma((len(LINE),)),
            dma((thirds,)), dma((thirds,)),
        ],
        compiler_params=pltpu.CompilerParams(
            collective_id=0, has_side_effects=True, vmem_limit_bytes=60 * 2**20
        ),
        name="layer",
    )(
        out_grad, mask_bits.T, send_rows[0], tile_row[0], tile_peer[0],
        node_feats, weight, tile_vals[0, 0],
    )


def solution(mesh):
    placed = (
        P("row", None),
        P("row", None),
        P("row", None),
        P(),
        P("row", None, None),
        P("row", "rep", None, None, None),
        P("row", "rep", None),
        P("row", "rep", None),
    )
    return jax.shard_map(
        local, mesh=mesh, in_specs=placed, out_specs=(P("row", None), P()), check_vma=False
    )
```

time: 398 us -> 76.5 us (0.19)
  waiting for transfers between devices: 119 us -> 0 us
  blocking collectives: 106 us -> 0 us
  matrix products: 63.1 us -> 0 us
  local copies, waits for them, and re-layouts: 45.7 us -> 3.93 us
  Pallas kernels: 42.9 us -> 71.7 us
  between operations: 14.8 us -> 0.64 us
    psum x1 -> x0, waiting for transfers between devices: 119 us -> none  [local(): w_sum = lax.psum(w_term, 'row')]
    psum x1 -> x0, blocking collectives: 106 us -> none  [local(): agg = lax.psum(partial_value, 'rep').astype(jnp.bfloat16)]
    dot_general x26 -> x0, matrix products: 63.1 us -> none  [the longest x8 23.5 us: add_block(): jnp.dot(peer_hot, flat_received, preferred_element_type=jnp.float32)]
    pallas_call x1, Pallas kernels: 42.9 us -> 71.7 us  [local(): pl.pallas_call(lambda *refs: kernel(scale, *refs), out_shape=(jax.ShapeDt...]
    while x16 -> x0, local copies, waits for them, and re-layouts: 23.4 us -> none
    dynamic_slice x16 -> x0, local copies, waits for them, and re-layouts: 12.1 us -> none  [the longest x8 6.07 us: add_block(): block_peers = lax.dynamic_slice_in_dim(peers, index * block, block, 0)]
    unnamed x11 -> x2, local copies, waits for them, and re-layouts: 8.6 us -> 3.93 us
  transfers between devices with their start and end apart: 1 -> 0, of which waited for: 1 -> 0; matrix products, arithmetic and copies ran while one was open for 0% -> 0% of each run, Pallas kernels for 0% -> 0%
where the time goes in v2:
time: 76.5 us; the launch traced here: 76.3 us
  Pallas kernels  71.7 us (94%)
  local copies, waits for them, and re-layouts  3.93 us (5%)
    pallas_call x1, Pallas kernels, local(): pl.pallas_call(lambda *refs: kernel(scale, *refs), out_shape=(jax.ShapeDt...  71.7 us
    unnamed x2, local copies, waits for them, and re-layouts  3.93 us

profile of v2, /device:TPU:1, one launch (start us, length us, event | category | flops | bytes accessed | tf_op | source)
XLA Modules:
  0.0 76.3 jit_solution(12766279701391757557)
XLA Ops:
  0.6 71.7 %layer.1 = (bf16[2048,256]{1,0:T(8,128)(2,1)}, f32[256,256]{1,0:T(8,128)}) custom-call(bf16[2048,256]{1,0:T(8,128)(2,1)} %refs_0_.1, s32[16,2048]{1,0:T(8,128)} %bitcast.6, s32[64,128]{1,0:T(8,128)} %bitcast.7, s32[1,512]{1,0:T(1,128)} %bitcast.8, s32[1,512]{1,0:T(1,128)} %bitcast.9, bf16[2048,256]{1,0:T(8,128)(2,1)} %refs_5_.1, bf16[256,256]{1,0:T(8,128)(2,1)} %refs_6_.1, ...), custom_call_target="tpu_custom_call" | custom-call | tf_op jit(solution)/shard_map/layer/pallas_call | solution.py:389
  72.3 2.3 %copy.12 = bf16[2048,256]{1,0:T(8,128)(2,1)} copy(bf16[2048,256]{1,0:T(8,128)(2,1)} %get-tuple-element.4) | data formatting | bytes 2097152
  74.6 1.7 %copy.13 = f32[256,256]{1,0:T(8,128)} copy(f32[256,256]{1,0:T(8,128)} %get-tuple-element.5) | data formatting | bytes 524288

commit v3 on v2

--- a/solution.py
+++ b/solution.py
@@ -12,29 +12,25 @@
 UORDER = (0, 7, 1, 6, 2, 5, 3, 4)
 GROUP = 4
 UNROLL = 20
+BATCH = 4
 PLANE = [(0, a, b) for a in range(4) for b in range(4) if (a, b) != (0, 0)]
 LINE = [(a, 0, 0) for a in range(1, 4)]
 
 
-def place(me):
-    return me % SIDE, me // (SIDE * SIDE), (me // SIDE) % SIDE
-
-
-def shifted(me, off, sign):
-    x, y, z = place(me)
-    dx, dy, dz = off
-    return (
-        ((y + sign * dy + SIDE) % SIDE) * SIDE + (z + sign * dz + SIDE) % SIDE
-    ) * SIDE + (x + sign * dx + SIDE) % SIDE
-
-
-def offset_of(i, u):
-    g, w = 7 - i, UORDER[u]
-    return (
-        g % 2 + 2 * (w & 1),
-        (g // 2) % 2 + 2 * ((w >> 1) & 1),
-        g // 4 + 2 * (w >> 2),
-    )
+def ring(v):
+    return [v] + [lax.rem(v + d, SIDE) for d in range(1, SIDE)]
+
+
+def group_rows(i, x, y, z, sign):
+    g = 7 - i
+    odd = (lax.rem(g, 2), lax.rem(lax.div(g, 2), 2), lax.div(g, 4))
+    at = [
+        [lax.rem(v + sign * o + SIDE, SIDE), lax.rem(v + sign * o + SIDE + 2, SIDE)]
+        for v, o in zip((x, y, z), odd)
+    ]
+    return [
+        at[1][(w >> 1) & 1] * (SIDE * SIDE) + at[2][w >> 2] * SIDE + at[0][w & 1] for w in UORDER
+    ]
 
 
 def iota(shape, dim):
@@ -87,10 +83,16 @@
     gp, listed, turned, wide, hot, sbuf, recv, table_v, table_s,
     steps, part, other, nft, ing, agg, term, red, line, done,
     in_sem, tv_sem, table_sem, own_sem, out_sem,
-    ssem, rsem, fssem, frsem, pssem, prsem, r1s, r1r, r2s, r2r, r3s, r3r,
+    near_sem, ssem, rsem, fssem, frsem, pssem, prsem, r1s, r1r, r2s, r2r, r3s, r3r, r4s, r4r,
 ):
     me = lax.axis_index("row")
     core = lax.axis_index("rep")
+    x, z, y = lax.rem(me, SIDE), lax.rem(lax.div(me, SIDE), SIDE), lax.div(me, SIDE * SIDE)
+    xs, ys, zs = ring(x), ring(y), ring(z)
+
+    def shifted(off):
+        return ys[off[1]] * (SIDE * SIDE) + zs[off[2]] * SIDE + xs[off[0]]
+
     rows, width = gp.shape
     peers, half = sbuf.shape[:2]
     tile = 2 * half
@@ -111,30 +113,30 @@
 
     barrier = pltpu.get_barrier_semaphore()
     pl.semaphore_signal(barrier, inc=1, device_id=sib, device_id_type=MESH)
-
-    @pl.loop(1, 64)
-    def _(j):
-        q = shifted(me, (j % 4, (j // 4) % 4, j // 16), 1)
-        pl.semaphore_signal(barrier, inc=1, device_id=(q, core), device_id_type=MESH)
-
-    for off in PLANE:
-        q = shifted(me, off, 1)
-        pl.semaphore_signal(barrier, inc=1, device_id=(q, 1 - core), device_id_type=MESH)
-    greeted = 1 + 63 + len(PLANE)
+    for off in LINE + PLANE:
+        pl.semaphore_signal(
+            barrier, inc=1, device_id=(shifted(off), core), device_id_type=MESH
+        )
+    greeted = 1 + len(LINE) + len(PLANE)
 
     loads[0].wait()
     listed[...] = jnp.full(listed.shape, -1, jnp.int32)
-    for u in range(8):
-
-        @pl.loop(0, 8)
-        def _(i, u=u):
-            q = shifted(me, offset_of(i, u), 1)
+
+    @pl.loop(0, 8)
+    def _(i):
+        for u, q in enumerate(group_rows(i, x, y, z, 1)):
             listed[pl.ds(i * 8 + u, 1), :] = sr[pl.ds(q, 1), :]
 
     turned[...] = listed[...].T
     mine = turned[pl.ds(pl.multiple_of(core * half, half), half), :]
     for j in range(64):
         wide[j] = jnp.broadcast_to(mine[:, j : j + 1], (half, 128))
+
+    pl.semaphore_wait(barrier, greeted)
+    for off in LINE:
+        pl.semaphore_signal(
+            near_sem, inc=1, device_id=(shifted(off), core), device_id_type=MESH
+        )
 
     words = mb.shape[0]
     feature = iota((2 * words, width), 1)
@@ -162,21 +164,17 @@
     lane = iota((half, 128), 1)
     halves = pl.ds(pl.multiple_of(core * half, half), half)
 
-    def send(i, u):
-        q = shifted(me, offset_of(i, u), 1)
-        j = i * 8 + u
+    def send(j, q):
         return pltpu.make_async_remote_copy(
             src_ref=sbuf.at[j], dst_ref=recv.at[me, halves],
-            send_sem=ssem.at[j], recv_sem=rsem.at[j],
+            send_sem=ssem, recv_sem=rsem.at[j],
             device_id=(q, core), device_id_type=MESH,
         )
 
-    def forward(i, u):
-        p = shifted(me, offset_of(i, u), -1)
-        j = i * 8 + u
+    def forward(p):
         return pltpu.make_async_remote_copy(
             src_ref=recv.at[p, halves], dst_ref=recv.at[p, halves],
-            send_sem=fssem.at[j], recv_sem=frsem.at[j],
+            send_sem=fssem, recv_sem=frsem,
             device_id=sib, device_id_type=MESH,
         )
 
@@ -185,34 +183,38 @@
 
     @pl.loop(0, 8)
     def _(i):
-        for u in range(8):
-            listed_at = wide[i * 8 + u]
-            block = listed_at >> 7
-            one = jnp.where((listed_at & 127) == lane, 1.0, 0.0)
-            for t in range(rows // 128):
-                hot[u * half : (u + 1) * half, t * 128 : (t + 1) * 128] = jnp.where(
-                    block == t, one, 0.0
-                ).astype(jnp.bfloat16)
-        picked = jnp.dot(hot[...], gp[...], preferred_element_type=jnp.float32)
-        for u in range(8):
-            sbuf[i * 8 + u] = picked[u * half : (u + 1) * half].astype(jnp.bfloat16)
-
-        @pl.when(i == 0)
-        def _():
-            pl.semaphore_wait(barrier, greeted)
-
-        for u in range(8):
-            if u == 0:
-
-                @pl.when(i < 7)
-                def _(u=u):
-                    send(i, u).start()
-
-                @pl.when(i == 7)
+        ahead = group_rows(i, x, y, z, 1)
+        for first in range(0, 8, BATCH):
+            for u in range(BATCH):
+                listed_at = wide[i * 8 + first + u]
+                block = listed_at >> 7
+                one = jnp.where((listed_at & 127) == lane, 1.0, 0.0)
+                for t in range(rows // 128):
+                    hot[u * half : (u + 1) * half, t * 128 : (t + 1) * 128] = jnp.where(
+                        block == t, one, 0.0
+                    ).astype(jnp.bfloat16)
+            picked = jnp.dot(hot[...], gp[...], preferred_element_type=jnp.float32)
+            for u in range(BATCH):
+                sbuf[i * 8 + first + u] = picked[u * half : (u + 1) * half].astype(jnp.bfloat16)
+
+            if first == 0:
+
+                @pl.when(i == 0)
                 def _():
-                    keep_own().start()
-            else:
-                send(i, u).start()
+                    pl.semaphore_wait(near_sem, len(LINE))
+
+            for u in range(first, first + BATCH):
+                if u == 0:
+
+                    @pl.when(i < 7)
+                    def _(u=u):
+                        send(i * 8 + u, ahead[u]).start()
+
+                    @pl.when(i == 7)
+                    def _():
+                        keep_own().start()
+                else:
+                    send(i * 8 + u, ahead[u]).start()
 
     fill = pltpu.make_async_copy(tv_hbm, tv, tv_sem)
     fill.start()
@@ -240,31 +242,28 @@
 
     @pl.loop(0, 8)
     def _(i):
-        for u in range(8):
+        for u, p in enumerate(group_rows(i, x, y, z, -1)):
             if u == 0:
 
                 @pl.when(i < 7)
-                def _(u=u):
-                    send(i, u).wait_recv()
+                def _(u=u, p=p):
+                    send(i * 8 + u, p).wait_recv()
 
                 @pl.when(i == 7)
                 def _():
                     keep_own().wait()
             else:
-                send(i, u).wait_recv()
-            forward(i, u).start()
-
-    @pl.loop(0, 8)
-    def _(i):
-        for u in range(8):
-            if u == 0:
-
-                @pl.when(i < 7)
-                def _(u=u):
-                    send(i, u).wait_send()
-            else:
-                send(i, u).wait_send()
-            forward(i, u).wait()
+                send(i * 8 + u, p).wait_recv()
+            forward(p).start()
+
+    def wait_bytes(like, send_sem, recv_sem):
+        return pltpu.make_async_remote_copy(
+            src_ref=like, dst_ref=like, send_sem=send_sem, recv_sem=recv_sem,
+            device_id=sib, device_id_type=MESH,
+        )
+
+    all_forwards = wait_bytes(sbuf, fssem, frsem)
+    all_forwards.wait_recv()
 
     fill.wait()
 
@@ -277,61 +276,40 @@
             prod = jnp.dot(left, right, preferred_element_type=jnp.float32)
             steps[g + 1] = jnp.where(table_s[2, g] == 1, steps[g], 0.0) + prod
 
-    def swap(r):
+    def swap(b):
+        at = pl.ds(b * GROUP, GROUP)
         return pltpu.make_async_remote_copy(
-            src_ref=part.at[r], dst_ref=other.at[r],
-            send_sem=pssem.at[r], recv_sem=prsem.at[r],
+            src_ref=part.at[at], dst_ref=other.at[at],
+            send_sem=pssem.at[b], recv_sem=prsem.at[b],
             device_id=sib, device_id_type=MESH,
         )
 
-    for r in range(row_tiles):
-        part[r] = steps[table_s[3, r]]
-        swap(r).start()
+    for b in range(row_tiles // GROUP):
+        for r in range(b * GROUP, (b + 1) * GROUP):
+            part[r] = steps[table_s[3, r]]
+        swap(b).start()
     term[...] = jnp.zeros(term.shape, term.dtype)
     for b in range(row_tiles // GROUP):
+        swap(b).wait_recv()
         for r in range(b * GROUP, (b + 1) * GROUP):
-            swap(r).wait()
             agg[r * tile : (r + 1) * tile, :] = (part[r] + other[r]).astype(jnp.bfloat16)
         at = slice(b * GROUP * tile, (b + 1) * GROUP * tile)
         left = jnp.concatenate([nft[b * GROUP + v] for v in range(GROUP)], axis=1)
         term[...] += jnp.dot(left, agg[at, :], preferred_element_type=jnp.float32)
 
-    x, y, z = place(me)
     spot = y * SIDE + z
     piece = red.shape[1]
 
     def rows_of(s):
         return pl.ds(pl.multiple_of(s * piece, piece), piece)
 
-    def first_send(n):
-        q = shifted(me, PLANE[n], 1)
-        return pltpu.make_async_remote_copy(
-            src_ref=term.at[rows_of(q // SIDE)], dst_ref=red.at[n],
-            send_sem=r1s.at[n], recv_sem=r1r.at[n],
-            device_id=(q, core), device_id_type=MESH,
-        )
-
-    def second_send(n):
-        return pltpu.make_async_remote_copy(
-            src_ref=line.at[x], dst_ref=line.at[x],
-            send_sem=r2s.at[n], recv_sem=r2r.at[n],
-            device_id=(shifted(me, LINE[n], 1), core), device_id_type=MESH,
-        )
-
-    def third_send(n):
-        if n < 2 * len(PLANE):
-            to = (shifted(me, PLANE[n // 2], 1), core if n % 2 == 0 else 1 - core)
-        else:
-            to = sib
-        at = pl.ds(pl.multiple_of(core * 128 + spot * piece, piece), piece)
-        return pltpu.make_async_remote_copy(
-            src_ref=done.at[at], dst_ref=done.at[at],
-            send_sem=r3s.at[n], recv_sem=r3r.at[n],
-            device_id=to, device_id_type=MESH,
-        )
-
-    for n in range(len(PLANE)):
-        first_send(n).start()
+    mine_at = pl.ds(pl.multiple_of(core * 128 + spot * piece, piece), piece)
+    for n, off in enumerate(PLANE):
+        q = shifted(off)
+        pltpu.make_async_remote_copy(
+            src_ref=term.at[rows_of(lax.div(q, SIDE))], dst_ref=red.at[n],
+            send_sem=r1s, recv_sem=r1r, device_id=(q, core), device_id_type=MESH,
+        ).start()
 
     @pl.loop(0, rows // 512)
     def _(b):
@@ -343,31 +321,65 @@
     out_copy = pltpu.make_async_copy(ing, ing_hbm, out_sem.at[0])
     out_copy.start()
     mine_sum = term[rows_of(spot), :]
+    first = wait_bytes(red, r1s, r1r)
+    first.wait_recv()
     for n in range(len(PLANE)):
-        first_send(n).wait_recv()
         mine_sum += red[n]
     line[x] = mine_sum
-    for n in range(len(LINE)):
-        second_send(n).start()
-    for n in range(len(LINE)):
-        second_send(n).wait_recv()
+    for off in LINE:
+        pltpu.make_async_remote_copy(
+            src_ref=line.at[x], dst_ref=line.at[x],
+            send_sem=r2s, recv_sem=r2r, device_id=(shifted(off), core), device_id_type=MESH,
+        ).start()
+    wait_bytes(sbuf.at[pl.ds(0, peers - 1)], ssem, ssem).wait_send()
+    all_forwards.wait_send()
+    for b in range(row_tiles // GROUP):
+        swap(b).wait_send()
+    first.wait_send()
+    second = wait_bytes(line.at[pl.ds(0, len(LINE))], r2s, r2r)
+    second.wait_recv()
     total = ((line[0] + line[1]) + line[2]) + line[3]
-    done[pl.ds(pl.multiple_of(core * 128 + spot * piece, piece), piece), :] = total * jnp.float32(scale)
-    thirds = 2 * len(PLANE) + 1
-    for n in range(thirds):
-        third_send(n).start()
-    for n in range(thirds):
-        third_send(n).wait_recv()
+    done[mine_at, :] = total * jnp.float32(scale)
+    for off in PLANE:
+        pltpu.make_async_remote_copy(
+            src_ref=done.at[mine_at], dst_ref=done.at[mine_at],
+            send_sem=r3s, recv_sem=r3r, device_id=(shifted(off), core), device_id_type=MESH,
+        ).start()
+    second.wait_send()
+    third = wait_bytes(red, r3s, r3r)
+    third.wait_recv()
+    mine_half = pl.ds(pl.multiple_of(core * 128, 128), 128)
+    fourth = pltpu.make_async_remote_copy(
+        src_ref=done.at[mine_half], dst_ref=done.at[mine_half],
+        send_sem=r4s, recv_sem=r4r, device_id=sib, device_id_type=MESH,
+    )
+    fourth.start()
+    third.wait_send()
+    fourth.wait()
     w_copy = pltpu.make_async_copy(done, wg_hbm, out_sem.at[1])
     w_copy.start()
-    for n in range(len(PLANE)):
-        first_send(n).wait_send()
-    for n in range(len(LINE)):
-        second_send(n).wait_send()
-    for n in range(thirds):
-        third_send(n).wait_send()
     out_copy.wait()
     w_copy.wait()
+
+
+def finish_kernel(ing_in, wg_in, ing_out, wg_out, ing, wg, in_sem, out_sem):
+    cuts = [(ing_in, ing, ing_out, pl.ds(n * 512, 512)) for n in range(ing.shape[0] // 512)]
+    cuts.append((wg_in, wg, wg_out, pl.ds(0, wg.shape[0])))
+    reads = [
+        pltpu.make_async_copy(src.at[at], mid.at[at], in_sem.at[n])
+        for n, (src, mid, _, at) in enumerate(cuts)
+    ]
+    writes = [
+        pltpu.make_async_copy(mid.at[at], dst.at[at], out_sem.at[n])
+        for n, (_, mid, dst, at) in enumerate(cuts)
+    ]
+    for read in reads:
+        read.start()
+    for read, write in zip(reads, writes):
+        read.wait()
+        write.start()
+    for write in writes:
+        write.wait()
 
 
 def local(node_feats, out_grad, mask_bits, weight, send_rows, tile_vals, tile_row, tile_peer):
@@ -385,13 +397,13 @@
     anywhere = pl.BlockSpec(memory_space=pl.ANY)
     bf16, f32, i32 = jnp.bfloat16, jnp.float32, jnp.int32
     dma = pltpu.SemaphoreType.DMA
-    thirds = 2 * len(PLANE) + 1
-    return pl.pallas_call(
+    parts_shape = (
+        jax.ShapeDtypeStruct((rows, width), bf16),
+        jax.ShapeDtypeStruct((width, width), f32),
+    )
+    parts = pl.pallas_call(
         lambda *refs: kernel(scale, *refs),
-        out_shape=(
-            jax.ShapeDtypeStruct((rows, width), bf16),
-            jax.ShapeDtypeStruct((width, width), f32),
-        ),
+        out_shape=parts_shape,
         in_specs=[anywhere] * 8,
         out_specs=(anywhere, anywhere),
         scratch_shapes=[
@@ -407,7 +419,7 @@
             pltpu.VMEM((128, 128), i32),
             pltpu.VMEM((128, 128), i32),
             pltpu.VMEM((peers, half, 128), i32),
-            pltpu.VMEM((8 * half, rows), bf16),
+            pltpu.VMEM((BATCH * half, rows), bf16),
             pltpu.VMEM((peers, half, width), bf16),
             pltpu.VMEM((peers + 1, tile, width), bf16),
             pltpu.VMEM((8, places), i32),
@@ -423,11 +435,9 @@
             pltpu.VMEM((SIDE, piece, width), f32),
             pltpu.VMEM((width, width), f32),
             dma((7,)), dma, dma, dma, dma((2,)),
-            dma((peers,)), dma((peers,)), dma((peers,)), dma((peers,)),
-            dma((row_tiles,)), dma((row_tiles,)),
-            dma((len(PLANE),)), dma((len(PLANE),)),
-            dma((len(LINE),)), dma((len(LINE),)),
-            dma((thirds,)), dma((thirds,)),
+            pltpu.SemaphoreType.REGULAR, dma, dma((peers,)), dma, dma,
+            dma((row_tiles // GROUP,)), dma((row_tiles // GROUP,)),
+            dma, dma, dma, dma, dma, dma, dma, dma,
         ],
         compiler_params=pltpu.CompilerParams(
             collective_id=0, has_side_effects=True, vmem_limit_bytes=60 * 2**20
@@ -437,6 +447,19 @@
         out_grad, mask_bits.T, send_rows[0], tile_row[0], tile_peer[0],
         node_feats, weight, tile_vals[0, 0],
     )
+    return pl.pallas_call(
+        finish_kernel,
+        out_shape=parts_shape,
+        in_specs=[anywhere] * 2,
+        out_specs=(anywhere, anywhere),
+        scratch_shapes=[
+            pltpu.VMEM((rows, width), bf16),
+            pltpu.VMEM((width, width), f32),
+            dma((rows // 512 + 1,)),
+            dma((rows // 512 + 1,)),
+        ],
+        name="finish",
+    )(*parts)
 
 
 def solution(mesh):

time: 76.5 us -> 68.4 us (0.89)
  Pallas kernels: 71.7 us -> 67.6 us
  local copies, waits for them, and re-layouts: 3.93 us -> 0 us
    pallas_call x1 -> x2, Pallas kernels: 71.7 us -> 67.6 us  [the longest x1 65.6 us: local(): pl.pallas_call(lambda *refs: kernel(scale, *refs), out_shape=parts_shape,...]
    unnamed x2 -> x0, local copies, waits for them, and re-layouts: 3.93 us -> none
where the time goes in v3:
time: 68.4 us; the launch traced here: 68.3 us
  Pallas kernels  67.6 us (99%)
    pallas_call x1, Pallas kernels, local(): pl.pallas_call(lambda *refs: kernel(scale, *refs), out_shape=parts_shape,...  65.6 us
    pallas_call x1, Pallas kernels, local(): pl.pallas_call(finish_kernel, out_shape=parts_shape, in_specs=[anywhere]...  2.08 us

profile of v3, /device:TPU:1, one launch (start us, length us, event | category | flops | bytes accessed | tf_op | source)
XLA Modules:
  0.0 68.3 jit_solution(18173712873698251139)
XLA Ops:
  0.6 65.6 %layer.1 = (bf16[2048,256]{1,0:T(8,128)(2,1)}, f32[256,256]{1,0:T(8,128)}) custom-call(bf16[2048,256]{1,0:T(8,128)(2,1)} %refs_0_.1, s32[16,2048]{1,0:T(8,128)} %bitcast.6, s32[64,128]{1,0:T(8,128)} %bitcast.7, s32[1,512]{1,0:T(1,128)} %bitcast.8, s32[1,512]{1,0:T(1,128)} %bitcast.9, bf16[2048,256]{1,0:T(8,128)(2,1)} %refs_5_.1, bf16[256,256]{1,0:T(8,128)(2,1)} %refs_6_.1, ...), custom_call_target="tpu_custom_call" | custom-call | tf_op jit(solution)/shard_map/layer/pallas_call | solution.py:404
  66.2 2.1 %finish.1 = (bf16[2048,256]{1,0:T(8,128)(2,1)}, f32[256,256]{1,0:T(8,128)}) custom-call(bf16[2048,256]{1,0:T(8,128)(2,1)} %get-tuple-element.4.ing_in, f32[256,256]{1,0:T(8,128)} %get-tuple-element.5.wg_in), custom_call_target="tpu_custom_call" | custom-call | tf_op jit(solution)/shard_map/finish/pallas_call | solution.py:450

commit v4 on v3

--- a/solution.py
+++ b/solution.py
@@ -21,11 +21,11 @@
     return [v] + [lax.rem(v + d, SIDE) for d in range(1, SIDE)]
 
 
-def group_rows(i, x, y, z, sign):
+def group_rows(i, x, y, z):
     g = 7 - i
     odd = (lax.rem(g, 2), lax.rem(lax.div(g, 2), 2), lax.div(g, 4))
     at = [
-        [lax.rem(v + sign * o + SIDE, SIDE), lax.rem(v + sign * o + SIDE + 2, SIDE)]
+        [lax.rem(v + o, SIDE), lax.rem(v + o + 2, SIDE)]
         for v, o in zip((x, y, z), odd)
     ]
     return [
@@ -35,6 +35,13 @@
 
 def iota(shape, dim):
     return lax.broadcasted_iota(jnp.int32, shape, dim)
+
+
+def place_of(peer, x, y, z):
+    dx, dy, dz = (x + 4 - (peer & 3)) & 3, (y + 4 - (peer >> 4)) & 3, (z + 4 - ((peer >> 2) & 3)) & 3
+    g = (dx & 1) + 2 * (dy & 1) + 4 * (dz & 1)
+    w = (dx >> 1) + 2 * (dy >> 1) + 4 * (dz >> 1)
+    return 8 * (7 - g) + jnp.where(w < 4, 2 * w, 15 - 2 * w)
 
 
 def layout_tables(row, peer, row_tiles, zero_peer, places):
@@ -83,7 +90,7 @@
     gp, listed, turned, wide, hot, sbuf, recv, table_v, table_s,
     steps, part, other, nft, ing, agg, term, red, line, done,
     in_sem, tv_sem, table_sem, own_sem, out_sem,
-    near_sem, ssem, rsem, fssem, frsem, pssem, prsem, r1s, r1r, r2s, r2r, r3s, r3r, r4s, r4r,
+    near_sem, ssem, rsem, fssem, frsem, pssem, prsem, r1s, r1r, r2s, r2r, r3s, r3r, r4s, r4r, r5s, r5r,
 ):
     me = lax.axis_index("row")
     core = lax.axis_index("rep")
@@ -124,7 +131,7 @@
 
     @pl.loop(0, 8)
     def _(i):
-        for u, q in enumerate(group_rows(i, x, y, z, 1)):
+        for u, q in enumerate(group_rows(i, x, y, z)):
             listed[pl.ds(i * 8 + u, 1), :] = sr[pl.ds(q, 1), :]
 
     turned[...] = listed[...].T
@@ -166,24 +173,23 @@
 
     def send(j, q):
         return pltpu.make_async_remote_copy(
-            src_ref=sbuf.at[j], dst_ref=recv.at[me, halves],
-            send_sem=ssem, recv_sem=rsem.at[j],
+            src_ref=sbuf.at[j], dst_ref=recv.at[j, halves],
+            send_sem=ssem, recv_sem=rsem.at[lax.div(j, 8)],
             device_id=(q, core), device_id_type=MESH,
         )
 
-    def forward(p):
+    def wait_bytes(like, send_sem, recv_sem):
         return pltpu.make_async_remote_copy(
-            src_ref=recv.at[p, halves], dst_ref=recv.at[p, halves],
-            send_sem=fssem, recv_sem=frsem,
+            src_ref=like, dst_ref=like, send_sem=send_sem, recv_sem=recv_sem,
             device_id=sib, device_id_type=MESH,
         )
 
     def keep_own():
-        return pltpu.make_async_copy(sbuf.at[peers - 8], recv.at[me, halves], own_sem)
+        return pltpu.make_async_copy(sbuf.at[peers - 8], recv.at[peers - 8, halves], own_sem)
 
     @pl.loop(0, 8)
     def _(i):
-        ahead = group_rows(i, x, y, z, 1)
+        ahead = group_rows(i, x, y, z)
         for first in range(0, 8, BATCH):
             for u in range(BATCH):
                 listed_at = wide[i * 8 + first + u]
@@ -223,7 +229,7 @@
     loads[3].wait()
     loads[4].wait()
     table_v[...] = layout_tables(
-        row_v[...], peer_v[...], row_tiles, peers, table_v.shape[1]
+        row_v[...], place_of(peer_v[...], x, y, z), row_tiles, peers, table_v.shape[1]
     )
     table_copy = pltpu.make_async_copy(table_v, table_s, table_sem)
     table_copy.start()
@@ -231,37 +237,25 @@
     steps[0] = jnp.zeros(steps.shape[1:], steps.dtype)
     loads[5].wait()
     loads[6].wait()
-    columns = pl.ds(pl.multiple_of(core * 128, 128), 128)
 
     @pl.loop(0, row_tiles)
     def _(r):
         at = pl.ds(pl.multiple_of(r * tile, tile), tile)
-        nft[r] = nf[at, columns].T
+        nft[r] = nf[at, :].T
 
     table_copy.wait()
 
-    @pl.loop(0, 8)
-    def _(i):
-        for u, p in enumerate(group_rows(i, x, y, z, -1)):
-            if u == 0:
-
-                @pl.when(i < 7)
-                def _(u=u, p=p):
-                    send(i * 8 + u, p).wait_recv()
-
-                @pl.when(i == 7)
-                def _():
-                    keep_own().wait()
-            else:
-                send(i * 8 + u, p).wait_recv()
-            forward(p).start()
-
-    def wait_bytes(like, send_sem, recv_sem):
-        return pltpu.make_async_remote_copy(
-            src_ref=like, dst_ref=like, send_sem=send_sem, recv_sem=recv_sem,
+    for i in range(8):
+        if i < 7:
+            wait_bytes(sbuf.at[pl.ds(0, 8)], ssem, rsem.at[i]).wait_recv()
+        else:
+            wait_bytes(sbuf.at[pl.ds(0, 7)], ssem, rsem.at[i]).wait_recv()
+            keep_own().wait()
+        here = recv.at[pl.ds(i * 8, 8), halves]
+        pltpu.make_async_remote_copy(
+            src_ref=here, dst_ref=here, send_sem=fssem, recv_sem=frsem,
             device_id=sib, device_id_type=MESH,
-        )
-
+        ).start()
     all_forwards = wait_bytes(sbuf, fssem, frsem)
     all_forwards.wait_recv()
 
@@ -276,6 +270,10 @@
             prod = jnp.dot(left, right, preferred_element_type=jnp.float32)
             steps[g + 1] = jnp.where(table_s[2, g] == 1, steps[g], 0.0) + prod
 
+    lanes = width // 2
+    mine_cols = pl.ds(pl.multiple_of(core * lanes, lanes), lanes)
+    sib_cols = pl.ds(pl.multiple_of((1 - core) * lanes, lanes), lanes)
+
     def swap(b):
         at = pl.ds(b * GROUP, GROUP)
         return pltpu.make_async_remote_copy(
@@ -286,92 +284,129 @@
 
     for b in range(row_tiles // GROUP):
         for r in range(b * GROUP, (b + 1) * GROUP):
-            part[r] = steps[table_s[3, r]]
+            part[r] = steps[table_s[3, r], :, sib_cols]
         swap(b).start()
     term[...] = jnp.zeros(term.shape, term.dtype)
     for b in range(row_tiles // GROUP):
         swap(b).wait_recv()
         for r in range(b * GROUP, (b + 1) * GROUP):
-            agg[r * tile : (r + 1) * tile, :] = (part[r] + other[r]).astype(jnp.bfloat16)
-        at = slice(b * GROUP * tile, (b + 1) * GROUP * tile)
+            mine_sum = steps[table_s[3, r], :, mine_cols] + other[r]
+            agg[core, r * tile : (r + 1) * tile, :] = mine_sum.astype(jnp.bfloat16)
         left = jnp.concatenate([nft[b * GROUP + v] for v in range(GROUP)], axis=1)
-        term[...] += jnp.dot(left, agg[at, :], preferred_element_type=jnp.float32)
-
-    spot = y * SIDE + z
+        right = agg[core, b * GROUP * tile : (b + 1) * GROUP * tile, :]
+        term[...] += jnp.dot(left, right, preferred_element_type=jnp.float32)
+
+    odds = [lax.rem(v, 2) for v in (x, y, z)]
+    ends = [lax.rem(lax.div(v + 1, 2), 2) for v in (x, y, z)]
     piece = red.shape[1]
 
     def rows_of(s):
         return pl.ds(pl.multiple_of(s * piece, piece), piece)
 
-    mine_at = pl.ds(pl.multiple_of(core * 128 + spot * piece, piece), piece)
-    for n, off in enumerate(PLANE):
-        q = shifted(off)
+    def in_cube(n):
+        bits = (n & 1, (n >> 1) & 1, n >> 2)
+        px, py, pz = [v + b * (1 - 2 * o) for v, o, b in zip((x, y, z), odds, bits)]
+        ox, oy, oz = [o + b * (1 - 2 * o) for o, b in zip(ends, bits)]
+        return py * (SIDE * SIDE) + pz * SIDE + px, ox + 2 * oy + 4 * oz
+
+    def facing(n):
+        bits = (n & 1, (n >> 1) & 1, n >> 2)
+        px, py, pz = [3 - v if b else v for v, b in zip((x, y, z), bits)]
+        return py * (SIDE * SIDE) + pz * SIDE + px
+
+    spot = in_cube(0)[1]
+    cube = lax.div(x, 2) + 2 * lax.div(y, 2) + 4 * lax.div(z, 2)
+    for n in range(1, 8):
+        q, to = in_cube(n)
         pltpu.make_async_remote_copy(
-            src_ref=term.at[rows_of(lax.div(q, SIDE))], dst_ref=red.at[n],
+            src_ref=term.at[rows_of(to)], dst_ref=red.at[n - 1],
             send_sem=r1s, recv_sem=r1r, device_id=(q, core), device_id_type=MESH,
         ).start()
+    give = pltpu.make_async_remote_copy(
+        src_ref=agg.at[core], dst_ref=agg.at[core],
+        send_sem=r5s, recv_sem=r5r, device_id=sib, device_id_type=MESH,
+    )
+    give.start()
+    mine_sum = term[rows_of(spot), :]
+    first = wait_bytes(red, r1s, r1r)
+    first.wait_recv()
+    for n in range(7):
+        mine_sum += red[n]
+    line[cube] = mine_sum
+    for n in range(1, 8):
+        pltpu.make_async_remote_copy(
+            src_ref=line.at[cube], dst_ref=line.at[cube],
+            send_sem=r2s, recv_sem=r2r, device_id=(facing(n), core), device_id_type=MESH,
+        ).start()
+
+    give.wait_recv()
 
     @pl.loop(0, rows // 512)
     def _(b):
         at = pl.ds(pl.multiple_of(b * 512, 512), 512)
-        ing[at, :] = lax.dot_general(
-            agg[at, :], wt[...], (((1,), (1,)), ((), ())), preferred_element_type=jnp.float32
-        ).astype(jnp.bfloat16)
+        total = sum(
+            lax.dot_general(
+                agg[h, at, :], wt[:, h * lanes : (h + 1) * lanes], (((1,), (1,)), ((), ())),
+                preferred_element_type=jnp.float32,
+            )
+            for h in range(2)
+        )
+        ing[at, :] = total.astype(jnp.bfloat16)
 
     out_copy = pltpu.make_async_copy(ing, ing_hbm, out_sem.at[0])
     out_copy.start()
-    mine_sum = term[rows_of(spot), :]
-    first = wait_bytes(red, r1s, r1r)
-    first.wait_recv()
-    for n in range(len(PLANE)):
-        mine_sum += red[n]
-    line[x] = mine_sum
-    for off in LINE:
+    second = wait_bytes(line.at[pl.ds(0, 7)], r2s, r2r)
+    second.wait_recv()
+    total = line[0]
+    for n in range(1, 8):
+        total += line[n]
+    done[core, rows_of(spot), :] = total * jnp.float32(scale)
+    for n in range(1, 8):
         pltpu.make_async_remote_copy(
-            src_ref=line.at[x], dst_ref=line.at[x],
-            send_sem=r2s, recv_sem=r2r, device_id=(shifted(off), core), device_id_type=MESH,
+            src_ref=done.at[core, rows_of(spot)], dst_ref=done.at[core, rows_of(spot)],
+            send_sem=r3s, recv_sem=r3r, device_id=(in_cube(n)[0], core), device_id_type=MESH,
         ).start()
     wait_bytes(sbuf.at[pl.ds(0, peers - 1)], ssem, ssem).wait_send()
     all_forwards.wait_send()
     for b in range(row_tiles // GROUP):
         swap(b).wait_send()
     first.wait_send()
-    second = wait_bytes(line.at[pl.ds(0, len(LINE))], r2s, r2r)
-    second.wait_recv()
-    total = ((line[0] + line[1]) + line[2]) + line[3]
-    done[mine_at, :] = total * jnp.float32(scale)
-    for off in PLANE:
-        pltpu.make_async_remote_copy(
-            src_ref=done.at[mine_at], dst_ref=done.at[mine_at],
-            send_sem=r3s, recv_sem=r3r, device_id=(shifted(off), core), device_id_type=MESH,
-        ).start()
     second.wait_send()
+    give.wait_send()
     third = wait_bytes(red, r3s, r3r)
     third.wait_recv()
-    mine_half = pl.ds(pl.multiple_of(core * 128, 128), 128)
     fourth = pltpu.make_async_remote_copy(
-        src_ref=done.at[mine_half], dst_ref=done.at[mine_half],
+        src_ref=done.at[core], dst_ref=done.at[core],
         send_sem=r4s, recv_sem=r4r, device_id=sib, device_id_type=MESH,
     )
     fourth.start()
+    mine_copy = pltpu.make_async_copy(done.at[core], wg_hbm.at[core], out_sem.at[1])
+    mine_copy.start()
     third.wait_send()
     fourth.wait()
-    w_copy = pltpu.make_async_copy(done, wg_hbm, out_sem.at[1])
-    w_copy.start()
+    sib_copy = pltpu.make_async_copy(done.at[1 - core], wg_hbm.at[1 - core], out_sem.at[2])
+    sib_copy.start()
     out_copy.wait()
-    w_copy.wait()
+    mine_copy.wait()
+    sib_copy.wait()
 
 
 def finish_kernel(ing_in, wg_in, ing_out, wg_out, ing, wg, in_sem, out_sem):
-    cuts = [(ing_in, ing, ing_out, pl.ds(n * 512, 512)) for n in range(ing.shape[0] // 512)]
-    cuts.append((wg_in, wg, wg_out, pl.ds(0, wg.shape[0])))
+    cuts = [
+        (ing_in.at[at], ing.at[at], ing_out.at[at])
+        for at in (pl.ds(n * 512, 512) for n in range(ing.shape[0] // 512))
+    ]
+    lanes = wg.shape[2]
+    cuts += [
+        (wg_in.at[h], wg.at[h], wg_out.at[:, pl.ds(h * lanes, lanes)]) for h in range(2)
+    ]
     reads = [
-        pltpu.make_async_copy(src.at[at], mid.at[at], in_sem.at[n])
-        for n, (src, mid, _, at) in enumerate(cuts)
+        pltpu.make_async_copy(src, mid, in_sem.at[n])
+        for n, (src, mid, _) in enumerate(cuts)
     ]
     writes = [
-        pltpu.make_async_copy(mid.at[at], dst.at[at], out_sem.at[n])
-        for n, (_, mid, dst, at) in enumerate(cuts)
+        pltpu.make_async_copy(mid, dst, out_sem.at[n])
+        for n, (_, mid, dst) in enumerate(cuts)
     ]
     for read in reads:
         read.start()
@@ -392,18 +427,16 @@
     most = -(-(slots + row_tiles * (GROUP - 1)) // GROUP)
     most = -(-most // UNROLL) * UNROLL
     places = -(-most * GROUP // 128) * 128
-    piece = width // 2 // 16
+    piece = width // 8
+    lanes = width // 2
     scale = 1.0 / math.sqrt(rows * lax.axis_size("row"))
     anywhere = pl.BlockSpec(memory_space=pl.ANY)
     bf16, f32, i32 = jnp.bfloat16, jnp.float32, jnp.int32
     dma = pltpu.SemaphoreType.DMA
-    parts_shape = (
-        jax.ShapeDtypeStruct((rows, width), bf16),
-        jax.ShapeDtypeStruct((width, width), f32),
-    )
+    in_shape = jax.ShapeDtypeStruct((rows, width), bf16)
     parts = pl.pallas_call(
         lambda *refs: kernel(scale, *refs),
-        out_shape=parts_shape,
+        out_shape=(in_shape, jax.ShapeDtypeStruct((2, width, lanes), f32)),
         in_specs=[anywhere] * 8,
         out_specs=(anywhere, anywhere),
         scratch_shapes=[
@@ -425,19 +458,19 @@
             pltpu.VMEM((8, places), i32),
             pltpu.SMEM((8, places), i32),
             pltpu.VMEM((most + 1, tile, width), f32),
-            pltpu.VMEM((row_tiles, tile, width), f32),
-            pltpu.VMEM((row_tiles, tile, width), f32),
-            pltpu.VMEM((row_tiles, width // 2, tile), bf16),
+            pltpu.VMEM((row_tiles, tile, lanes), f32),
+            pltpu.VMEM((row_tiles, tile, lanes), f32),
+            pltpu.VMEM((row_tiles, width, tile), bf16),
             pltpu.VMEM((rows, width), bf16),
-            pltpu.VMEM((rows, width), bf16),
-            pltpu.VMEM((width // 2, width), f32),
-            pltpu.VMEM((len(PLANE), piece, width), f32),
-            pltpu.VMEM((SIDE, piece, width), f32),
-            pltpu.VMEM((width, width), f32),
-            dma((7,)), dma, dma, dma, dma((2,)),
-            pltpu.SemaphoreType.REGULAR, dma, dma((peers,)), dma, dma,
+            pltpu.VMEM((2, rows, lanes), bf16),
+            pltpu.VMEM((width, lanes), f32),
+            pltpu.VMEM((7, piece, lanes), f32),
+            pltpu.VMEM((8, piece, lanes), f32),
+            pltpu.VMEM((2, width, lanes), f32),
+            dma((7,)), dma, dma, dma, dma((3,)),
+            pltpu.SemaphoreType.REGULAR, dma, dma((8,)), dma, dma,
             dma((row_tiles // GROUP,)), dma((row_tiles // GROUP,)),
-            dma, dma, dma, dma, dma, dma, dma, dma,
+            dma, dma, dma, dma, dma, dma, dma, dma, dma, dma,
         ],
         compiler_params=pltpu.CompilerParams(
             collective_id=0, has_side_effects=True, vmem_limit_bytes=60 * 2**20
@@ -449,14 +482,14 @@
     )
     return pl.pallas_call(
         finish_kernel,
-        out_shape=parts_shape,
+        out_shape=(in_shape, jax.ShapeDtypeStruct((width, width), f32)),
         in_specs=[anywhere] * 2,
         out_specs=(anywhere, anywhere),
         scratch_shapes=[
             pltpu.VMEM((rows, width), bf16),
-            pltpu.VMEM((width, width), f32),
-            dma((rows // 512 + 1,)),
-            dma((rows // 512 + 1,)),
+            pltpu.VMEM((2, width, lanes), f32),
+            dma((rows // 512 + 2,)),
+            dma((rows // 512 + 2,)),
         ],
         name="finish",
     )(*parts)

time: 68.4 us -> 65.6 us (0.959)
  Pallas kernels: 67.6 us -> 64.8 us
    pallas_call x2, Pallas kernels: 67.6 us -> 64.8 us  [the longest x1 62.7 us: local(): pl.pallas_call(lambda *refs: kernel(scale, *refs), out_shape=(in_shape, j...]
where the time goes in v4:
time: 65.6 us; the launch traced here: 65.5 us
  Pallas kernels  64.8 us (99%)
    pallas_call x1, Pallas kernels, local(): pl.pallas_call(lambda *refs: kernel(scale, *refs), out_shape=(in_shape, j...  62.7 us
    pallas_call x1, Pallas kernels, local(): pl.pallas_call(finish_kernel, out_shape=(in_shape, jax.ShapeDtypeStruct((...  2.1 us

profile of v4, /device:TPU:1, one launch (start us, length us, event | category | flops | bytes accessed | tf_op | source)
XLA Modules:
  0.0 65.5 jit_solution(6488676545155211753)
XLA Ops:
  0.6 62.7 %layer.1 = (bf16[2048,256]{1,0:T(8,128)(2,1)}, f32[2,256,128]{2,1,0:T(8,128)}) custom-call(bf16[2048,256]{1,0:T(8,128)(2,1)} %refs_0_.1, s32[16,2048]{1,0:T(8,128)} %bitcast.6, s32[64,128]{1,0:T(8,128)} %bitcast.7, s32[1,512]{1,0:T(1,128)} %bitcast.8, s32[1,512]{1,0:T(1,128)} %bitcast.9, bf16[2048,256]{1,0:T(8,128)(2,1)} %refs_5_.1, ...), custom_call_target="tpu_custom_call" | custom-call | tf_op jit(solution)/shard_map/layer/pallas_call | solution.py:437
  63.4 2.1 %finish.1 = (bf16[2048,256]{1,0:T(8,128)(2,1)}, f32[256,256]{1,0:T(8,128)}) custom-call(bf16[2048,256]{1,0:T(8,128)(2,1)} %get-tuple-element.4.ing_in, f32[2,256,128]{2,1,0:T(8,128)} %get-tuple-element.5.wg_in), custom_call_target="tpu_custom_call" | custom-call | tf_op jit(solution)/shard_map/finish/pallas_call | solution.py:483

commit v5 on v4

--- a/solution.py
+++ b/solution.py
@@ -10,9 +10,9 @@
 MESH = pl.DeviceIdType.MESH
 SIDE = 4
 UORDER = (0, 7, 1, 6, 2, 5, 3, 4)
-GROUP = 4
-UNROLL = 20
-BATCH = 4
+GROUP = 8
+CHUNK = 4
+UNROLL = 40
 PLANE = [(0, a, b) for a in range(4) for b in range(4) if (a, b) != (0, 0)]
 LINE = [(a, 0, 0) for a in range(1, 4)]
 
@@ -87,8 +87,8 @@
     og_hbm, mb_hbm, sr_hbm, row_hbm, peer_hbm, nf_hbm, wt_hbm, tv_hbm,
     ing_hbm, wg_hbm,
     og, mb, sr, row_v, peer_v, nf, wt, tv,
-    gp, listed, turned, wide, hot, sbuf, recv, table_v, table_s,
-    steps, part, other, nft, ing, agg, term, red, line, done,
+    gp, listed, turned, wide, hot, sbuf, recv_a, recv_b, table_v, table_s,
+    later, steps, sums, part, other, nft, ing, agg, term, red, line, done,
     in_sem, tv_sem, table_sem, own_sem, out_sem,
     near_sem, ssem, rsem, fssem, frsem, pssem, prsem, r1s, r1r, r2s, r2r, r3s, r3r, r4s, r4r, r5s, r5r,
 ):
@@ -101,8 +101,10 @@
         return ys[off[1]] * (SIDE * SIDE) + zs[off[2]] * SIDE + xs[off[0]]
 
     rows, width = gp.shape
-    peers, half = sbuf.shape[:2]
+    peers, quarter = sbuf.shape[1:3]
+    half = 2 * quarter
     tile = 2 * half
+    recv = (recv_a, recv_b)
     row_tiles = rows // tile
     sib = (me, 1 - core)
 
@@ -135,7 +137,13 @@
             listed[pl.ds(i * 8 + u, 1), :] = sr[pl.ds(q, 1), :]
 
     turned[...] = listed[...].T
-    mine = turned[pl.ds(pl.multiple_of(core * half, half), half), :]
+    mine = jnp.concatenate(
+        [
+            turned[pl.ds(pl.multiple_of(ph * half + core * quarter, quarter), quarter), :]
+            for ph in range(2)
+        ],
+        axis=0,
+    )
     for j in range(64):
         wide[j] = jnp.broadcast_to(mine[:, j : j + 1], (half, 128))
 
@@ -168,13 +176,14 @@
         grad = og[at, :].astype(jnp.float32)
         gp[at, :] = jnp.where(keep == 1, grad, 0.0).astype(jnp.bfloat16)
 
-    lane = iota((half, 128), 1)
-    halves = pl.ds(pl.multiple_of(core * half, half), half)
-
-    def send(j, q):
+    lane = iota((quarter, 128), 1)
+    mine_rows = pl.ds(pl.multiple_of(core * quarter, quarter), quarter)
+
+    def send(ph, t, u, q):
         return pltpu.make_async_remote_copy(
-            src_ref=sbuf.at[j], dst_ref=recv.at[j, halves],
-            send_sem=ssem, recv_sem=rsem.at[lax.div(j, 8)],
+            src_ref=sbuf.at[ph, (t - 8 * ph) * 8 + u],
+            dst_ref=recv[ph].at[(t - 8 * ph) * 8 + u, mine_rows],
+            send_sem=ssem, recv_sem=rsem.at[t],
             device_id=(q, core), device_id_type=MESH,
         )
 
@@ -184,43 +193,43 @@
             device_id=sib, device_id_type=MESH,
         )
 
-    def keep_own():
-        return pltpu.make_async_copy(sbuf.at[peers - 8], recv.at[peers - 8, halves], own_sem)
-
-    @pl.loop(0, 8)
-    def _(i):
-        ahead = group_rows(i, x, y, z)
-        for first in range(0, 8, BATCH):
-            for u in range(BATCH):
-                listed_at = wide[i * 8 + first + u]
+    def keep_own(ph):
+        return pltpu.make_async_copy(
+            sbuf.at[ph, peers - 8], recv[ph].at[peers - 8, mine_rows], own_sem.at[ph]
+        )
+
+    for ph in range(2):
+
+        @pl.loop(8 * ph, 8 * ph + 8)
+        def _(t, ph=ph):
+            i = t - 8 * ph
+            ahead = group_rows(i, x, y, z)
+            for u in range(8):
+                listed_at = wide[i * 8 + u, ph * quarter : (ph + 1) * quarter]
                 block = listed_at >> 7
                 one = jnp.where((listed_at & 127) == lane, 1.0, 0.0)
-                for t in range(rows // 128):
-                    hot[u * half : (u + 1) * half, t * 128 : (t + 1) * 128] = jnp.where(
-                        block == t, one, 0.0
+                for c in range(rows // 128):
+                    hot[u * quarter : (u + 1) * quarter, c * 128 : (c + 1) * 128] = jnp.where(
+                        block == c, one, 0.0
                     ).astype(jnp.bfloat16)
             picked = jnp.dot(hot[...], gp[...], preferred_element_type=jnp.float32)
-            for u in range(BATCH):
-                sbuf[i * 8 + first + u] = picked[u * half : (u + 1) * half].astype(jnp.bfloat16)
-
-            if first == 0:
-
-                @pl.when(i == 0)
-                def _():
-                    pl.semaphore_wait(near_sem, len(LINE))
-
-            for u in range(first, first + BATCH):
-                if u == 0:
-
-                    @pl.when(i < 7)
-                    def _(u=u):
-                        send(i * 8 + u, ahead[u]).start()
-
-                    @pl.when(i == 7)
-                    def _():
-                        keep_own().start()
-                else:
-                    send(i * 8 + u, ahead[u]).start()
+            for u in range(8):
+                sbuf[ph, i * 8 + u] = picked[u * quarter : (u + 1) * quarter].astype(jnp.bfloat16)
+
+            @pl.when(t == 0)
+            def _():
+                pl.semaphore_wait(near_sem, len(LINE))
+
+            @pl.when(i < 7)
+            def _():
+                send(ph, t, 0, ahead[0]).start()
+
+            @pl.when(i == 7)
+            def _():
+                keep_own(ph).start()
+
+            for u in range(1, 8):
+                send(ph, t, u, ahead[u]).start()
 
     fill = pltpu.make_async_copy(tv_hbm, tv, tv_sem)
     fill.start()
@@ -233,7 +242,8 @@
     )
     table_copy = pltpu.make_async_copy(table_v, table_s, table_sem)
     table_copy.start()
-    recv[peers] = jnp.zeros(recv.shape[1:], recv.dtype)
+    for buf in recv:
+        buf[peers] = jnp.zeros(buf.shape[1:], buf.dtype)
     steps[0] = jnp.zeros(steps.shape[1:], steps.dtype)
     loads[5].wait()
     loads[6].wait()
@@ -245,55 +255,76 @@
 
     table_copy.wait()
 
-    for i in range(8):
-        if i < 7:
-            wait_bytes(sbuf.at[pl.ds(0, 8)], ssem, rsem.at[i]).wait_recv()
-        else:
-            wait_bytes(sbuf.at[pl.ds(0, 7)], ssem, rsem.at[i]).wait_recv()
-            keep_own().wait()
-        here = recv.at[pl.ds(i * 8, 8), halves]
-        pltpu.make_async_remote_copy(
-            src_ref=here, dst_ref=here, send_sem=fssem, recv_sem=frsem,
-            device_id=sib, device_id_type=MESH,
-        ).start()
-    all_forwards = wait_bytes(sbuf, fssem, frsem)
-    all_forwards.wait_recv()
-
+    def take(ph, groups):
+        for i in groups:
+            lists = 8 if i < 7 else 7
+            wait_bytes(sbuf.at[0, pl.ds(0, lists)], ssem, rsem.at[8 * ph + i]).wait_recv()
+            if i == 7:
+                keep_own(ph).wait()
+            here = recv[ph].at[pl.ds(i * 8, 8), mine_rows]
+            pltpu.make_async_remote_copy(
+                src_ref=here, dst_ref=here, send_sem=fssem.at[ph], recv_sem=frsem.at[ph],
+                device_id=sib, device_id_type=MESH,
+            ).start()
+
+    def taken(ph):
+        wait_bytes(sbuf.at[0], fssem.at[ph], frsem.at[ph]).wait_recv()
+
+    def products(ph, start, stop):
+        @pl.loop(start, stop)
+        def _(i):
+            for n in range(UNROLL):
+                g = i * UNROLL + n
+                if ph == 0:
+                    tiles = [tv[table_s[0, GROUP * g + v]] for v in range(GROUP)]
+                    left = jnp.concatenate([t[:, :half] for t in tiles], axis=1)
+                    later[g] = jnp.concatenate([t[:, half:] for t in tiles], axis=1)
+                else:
+                    left = later[g]
+                right = jnp.concatenate(
+                    [recv[ph][table_s[1, GROUP * g + v]] for v in range(GROUP)], axis=0
+                )
+                prod = jnp.dot(left, right, preferred_element_type=jnp.float32)
+                steps[g + 1] = jnp.where(table_s[2, g] == 1, steps[g], 0.0) + prod
+
+    loops = (steps.shape[0] - 1) // UNROLL
+    take(0, range(8))
+    taken(0)
     fill.wait()
-
-    @pl.loop(0, (steps.shape[0] - 1) // UNROLL)
-    def _(i):
-        for u in range(UNROLL):
-            g = i * UNROLL + u
-            left = jnp.concatenate([tv[table_s[0, GROUP * g + v]] for v in range(GROUP)], axis=1)
-            right = jnp.concatenate([recv[table_s[1, GROUP * g + v]] for v in range(GROUP)], axis=0)
-            prod = jnp.dot(left, right, preferred_element_type=jnp.float32)
-            steps[g + 1] = jnp.where(table_s[2, g] == 1, steps[g], 0.0) + prod
+    products(0, 0, loops // 2)
+    take(1, range(4))
+    products(0, loops // 2, loops)
+    for r in range(row_tiles):
+        sums[r] = steps[table_s[3, r]]
+    take(1, range(4, 8))
+    taken(1)
+    products(1, 0, loops)
 
     lanes = width // 2
     mine_cols = pl.ds(pl.multiple_of(core * lanes, lanes), lanes)
     sib_cols = pl.ds(pl.multiple_of((1 - core) * lanes, lanes), lanes)
 
     def swap(b):
-        at = pl.ds(b * GROUP, GROUP)
+        at = pl.ds(b * CHUNK, CHUNK)
         return pltpu.make_async_remote_copy(
             src_ref=part.at[at], dst_ref=other.at[at],
             send_sem=pssem.at[b], recv_sem=prsem.at[b],
             device_id=sib, device_id_type=MESH,
         )
 
-    for b in range(row_tiles // GROUP):
-        for r in range(b * GROUP, (b + 1) * GROUP):
-            part[r] = steps[table_s[3, r], :, sib_cols]
+    for b in range(row_tiles // CHUNK):
+        for r in range(b * CHUNK, (b + 1) * CHUNK):
+            part[r] = sums[r, :, sib_cols] + steps[table_s[3, r], :, sib_cols]
         swap(b).start()
     term[...] = jnp.zeros(term.shape, term.dtype)
-    for b in range(row_tiles // GROUP):
+    for b in range(row_tiles // CHUNK):
         swap(b).wait_recv()
-        for r in range(b * GROUP, (b + 1) * GROUP):
-            mine_sum = steps[table_s[3, r], :, mine_cols] + other[r]
+        for r in range(b * CHUNK, (b + 1) * CHUNK):
+            mine_sum = sums[r, :, mine_cols] + steps[table_s[3, r], :, mine_cols]
+            mine_sum += other[r]
             agg[core, r * tile : (r + 1) * tile, :] = mine_sum.astype(jnp.bfloat16)
-        left = jnp.concatenate([nft[b * GROUP + v] for v in range(GROUP)], axis=1)
-        right = agg[core, b * GROUP * tile : (b + 1) * GROUP * tile, :]
+        left = jnp.concatenate([nft[b * CHUNK + v] for v in range(CHUNK)], axis=1)
+        right = agg[core, b * CHUNK * tile : (b + 1) * CHUNK * tile, :]
         term[...] += jnp.dot(left, right, preferred_element_type=jnp.float32)
 
     odds = [lax.rem(v, 2) for v in (x, y, z)]
@@ -366,9 +397,10 @@
             src_ref=done.at[core, rows_of(spot)], dst_ref=done.at[core, rows_of(spot)],
             send_sem=r3s, recv_sem=r3r, device_id=(in_cube(n)[0], core), device_id_type=MESH,
         ).start()
-    wait_bytes(sbuf.at[pl.ds(0, peers - 1)], ssem, ssem).wait_send()
-    all_forwards.wait_send()
-    for b in range(row_tiles // GROUP):
+    for ph in range(2):
+        wait_bytes(sbuf.at[ph, pl.ds(0, peers - 1)], ssem, ssem).wait_send()
+        wait_bytes(sbuf.at[ph], fssem.at[ph], frsem.at[ph]).wait_send()
+    for b in range(row_tiles // CHUNK):
         swap(b).wait_send()
     first.wait_send()
     second.wait_send()
@@ -452,12 +484,15 @@
             pltpu.VMEM((128, 128), i32),
             pltpu.VMEM((128, 128), i32),
             pltpu.VMEM((peers, half, 128), i32),
-            pltpu.VMEM((BATCH * half, rows), bf16),
-            pltpu.VMEM((peers, half, width), bf16),
-            pltpu.VMEM((peers + 1, tile, width), bf16),
+            pltpu.VMEM((4 * half, rows), bf16),
+            pltpu.VMEM((2, peers, half // 2, width), bf16),
+            pltpu.VMEM((peers + 1, half, width), bf16),
+            pltpu.VMEM((peers + 1, half, width), bf16),
             pltpu.VMEM((8, places), i32),
             pltpu.SMEM((8, places), i32),
+            pltpu.VMEM((most, tile, GROUP * half), bf16),
             pltpu.VMEM((most + 1, tile, width), f32),
+            pltpu.VMEM((row_tiles, tile, width), f32),
             pltpu.VMEM((row_tiles, tile, lanes), f32),
             pltpu.VMEM((row_tiles, tile, lanes), f32),
             pltpu.VMEM((row_tiles, width, tile), bf16),
@@ -467,9 +502,9 @@
             pltpu.VMEM((7, piece, lanes), f32),
             pltpu.VMEM((8, piece, lanes), f32),
             pltpu.VMEM((2, width, lanes), f32),
-            dma((7,)), dma, dma, dma, dma((3,)),
-            pltpu.SemaphoreType.REGULAR, dma, dma((8,)), dma, dma,
-            dma((row_tiles // GROUP,)), dma((row_tiles // GROUP,)),
+            dma((7,)), dma, dma, dma((2,)), dma((3,)),
+            pltpu.SemaphoreType.REGULAR, dma, dma((16,)), dma((2,)), dma((2,)),
+            dma((row_tiles // CHUNK,)), dma((row_tiles // CHUNK,)),
             dma, dma, dma, dma, dma, dma, dma, dma, dma, dma,
         ],
         compiler_params=pltpu.CompilerParams(

time: 65.6 us -> 63.1 us (0.962)
  Pallas kernels: 64.8 us -> 62.3 us
    pallas_call x1, Pallas kernels: 62.7 us -> 60.2 us  [local(): pl.pallas_call(lambda *refs: kernel(scale, *refs), out_shape=(in_shape, j...]
where the time goes in v5:
time: 63.1 us; the launch traced here: 62.9 us
  Pallas kernels  62.3 us (99%)
  between operations  0.64 us (1%)
    pallas_call x1, Pallas kernels, local(): pl.pallas_call(lambda *refs: kernel(scale, *refs), out_shape=(in_shape, j...  60.2 us
    pallas_call x1, Pallas kernels, local(): pl.pallas_call(finish_kernel, out_shape=(in_shape, jax.ShapeDtypeStruct((...  2.1 us

profile of v5, /device:TPU:1, one launch (start us, length us, event | category | flops | bytes accessed | tf_op | source)
XLA Modules:
  0.0 62.9 jit_solution(10097737011238864498)
XLA Ops:
  0.6 60.2 %layer.1 = (bf16[2048,256]{1,0:T(8,128)(2,1)}, f32[2,256,128]{2,1,0:T(8,128)}) custom-call(bf16[2048,256]{1,0:T(8,128)(2,1)} %refs_0_.1, s32[16,2048]{1,0:T(8,128)} %bitcast.6, s32[64,128]{1,0:T(8,128)} %bitcast.7, s32[1,512]{1,0:T(1,128)} %bitcast.8, s32[1,512]{1,0:T(1,128)} %bitcast.9, bf16[2048,256]{1,0:T(8,128)(2,1)} %refs_5_.1, ...), custom_call_target="tpu_custom_call" | custom-call | tf_op jit(solution)/shard_map/layer/pallas_call | solution.py:469
  60.8 2.1 %finish.1 = (bf16[2048,256]{1,0:T(8,128)(2,1)}, f32[256,256]{1,0:T(8,128)}) custom-call(bf16[2048,256]{1,0:T(8,128)(2,1)} %get-tuple-element.4.ing_in, f32[2,256,128]{2,1,0:T(8,128)} %get-tuple-element.5.wg_in), custom_call_target="tpu_custom_call" | custom-call | tf_op jit(solution)/shard_map/finish/pallas_call | solution.py:518

commit v6 on v5

--- a/solution.py
+++ b/solution.py
@@ -392,11 +392,17 @@
     for n in range(1, 8):
         total += line[n]
     done[core, rows_of(spot), :] = total * jnp.float32(scale)
+    def hand_out(to, send_sem, recv_sem):
+        here = done.at[core, rows_of(spot)]
+        pltpu.make_async_remote_copy(
+            src_ref=here, dst_ref=here, send_sem=send_sem, recv_sem=recv_sem,
+            device_id=to, device_id_type=MESH,
+        ).start()
+
     for n in range(1, 8):
-        pltpu.make_async_remote_copy(
-            src_ref=done.at[core, rows_of(spot)], dst_ref=done.at[core, rows_of(spot)],
-            send_sem=r3s, recv_sem=r3r, device_id=(in_cube(n)[0], core), device_id_type=MESH,
-        ).start()
+        hand_out((in_cube(n)[0], core), r3s, r3r)
+        hand_out((in_cube(n)[0], 1 - core), r4s, r4r)
+    hand_out(sib, r4s, r4r)
     for ph in range(2):
         wait_bytes(sbuf.at[ph, pl.ds(0, peers - 1)], ssem, ssem).wait_send()
         wait_bytes(sbuf.at[ph], fssem.at[ph], frsem.at[ph]).wait_send()
@@ -407,11 +413,7 @@
     give.wait_send()
     third = wait_bytes(red, r3s, r3r)
     third.wait_recv()
-    fourth = pltpu.make_async_remote_copy(
-        src_ref=done.at[core], dst_ref=done.at[core],
-        send_sem=r4s, recv_sem=r4r, device_id=sib, device_id_type=MESH,
-    )
-    fourth.start()
+    fourth = wait_bytes(line, r4s, r4r)
     mine_copy = pltpu.make_async_copy(done.at[core], wg_hbm.at[core], out_sem.at[1])
     mine_copy.start()
     third.wait_send()

time: 63.1 us -> 62.5 us (level)
  no operation moved by 1% of the time
where the time goes in v6:
time: 62.5 us; the launch traced here: 62.3 us
  Pallas kernels  61.7 us (99%)
  between operations  0.64 us (1%)
    pallas_call x1, Pallas kernels, local(): pl.pallas_call(lambda *refs: kernel(scale, *refs), out_shape=(in_shape, j...  59.6 us
    pallas_call x1, Pallas kernels, local(): pl.pallas_call(finish_kernel, out_shape=(in_shape, jax.ShapeDtypeStruct((...  2.1 us

profile of v6, /device:TPU:1, one launch (start us, length us, event | category | flops | bytes accessed | tf_op | source)
XLA Modules:
  0.0 62.3 jit_solution(2937673488409067971)
XLA Ops:
  0.6 59.6 %layer.1 = (bf16[2048,256]{1,0:T(8,128)(2,1)}, f32[2,256,128]{2,1,0:T(8,128)}) custom-call(bf16[2048,256]{1,0:T(8,128)(2,1)} %refs_0_.1, s32[16,2048]{1,0:T(8,128)} %bitcast.6, s32[64,128]{1,0:T(8,128)} %bitcast.7, s32[1,512]{1,0:T(1,128)} %bitcast.8, s32[1,512]{1,0:T(1,128)} %bitcast.9, bf16[2048,256]{1,0:T(8,128)(2,1)} %refs_5_.1, ...), custom_call_target="tpu_custom_call" | custom-call | tf_op jit(solution)/shard_map/layer/pallas_call | solution.py:471
  60.2 2.1 %finish.1 = (bf16[2048,256]{1,0:T(8,128)(2,1)}, f32[256,256]{1,0:T(8,128)}) custom-call(bf16[2048,256]{1,0:T(8,128)(2,1)} %get-tuple-element.4.ing_in, f32[2,256,128]{2,1,0:T(8,128)} %get-tuple-element.5.wg_in), custom_call_target="tpu_custom_call" | custom-call | tf_op jit(solution)/shard_map/finish/pallas_call | solution.py:520

commit v7 on v6

--- a/solution.py
+++ b/solution.py
@@ -15,6 +15,7 @@
 UNROLL = 40
 PLANE = [(0, a, b) for a in range(4) for b in range(4) if (a, b) != (0, 0)]
 LINE = [(a, 0, 0) for a in range(1, 4)]
+FAR_FIRST = (7, 6, 5, 3, 4, 2, 1)
 
 
 def ring(v):
@@ -347,7 +348,7 @@
 
     spot = in_cube(0)[1]
     cube = lax.div(x, 2) + 2 * lax.div(y, 2) + 4 * lax.div(z, 2)
-    for n in range(1, 8):
+    for n in FAR_FIRST:
         q, to = in_cube(n)
         pltpu.make_async_remote_copy(
             src_ref=term.at[rows_of(to)], dst_ref=red.at[n - 1],
@@ -364,7 +365,7 @@
     for n in range(7):
         mine_sum += red[n]
     line[cube] = mine_sum
-    for n in range(1, 8):
+    for n in FAR_FIRST:
         pltpu.make_async_remote_copy(
             src_ref=line.at[cube], dst_ref=line.at[cube],
             send_sem=r2s, recv_sem=r2r, device_id=(facing(n), core), device_id_type=MESH,
@@ -399,7 +400,7 @@
             device_id=to, device_id_type=MESH,
         ).start()
 
-    for n in range(1, 8):
+    for n in FAR_FIRST:
         hand_out((in_cube(n)[0], core), r3s, r3r)
         hand_out((in_cube(n)[0], 1 - core), r4s, r4r)
     hand_out(sib, r4s, r4r)

time: 62.5 us -> 62.3 us (level)
  no operation moved by 1% of the time
where the time goes in v7:
time: 62.3 us; the launch traced here: 62.1 us
  Pallas kernels  61.5 us (99%)
  between operations  0.64 us (1%)
    pallas_call x1, Pallas kernels, local(): pl.pallas_call(lambda *refs: kernel(scale, *refs), out_shape=(in_shape, j...  59.4 us
    pallas_call x1, Pallas kernels, local(): pl.pallas_call(finish_kernel, out_shape=(in_shape, jax.ShapeDtypeStruct((...  2.1 us

profile of v7, /device:TPU:1, one launch (start us, length us, event | category | flops | bytes accessed | tf_op | source)
XLA Modules:
  0.0 62.1 jit_solution(18409566126938068151)
XLA Ops:
  0.6 59.4 %layer.1 = (bf16[2048,256]{1,0:T(8,128)(2,1)}, f32[2,256,128]{2,1,0:T(8,128)}) custom-call(bf16[2048,256]{1,0:T(8,128)(2,1)} %refs_0_.1, s32[16,2048]{1,0:T(8,128)} %bitcast.6, s32[64,128]{1,0:T(8,128)} %bitcast.7, s32[1,512]{1,0:T(1,128)} %bitcast.8, s32[1,512]{1,0:T(1,128)} %bitcast.9, bf16[2048,256]{1,0:T(8,128)(2,1)} %refs_5_.1, ...), custom_call_target="tpu_custom_call" | custom-call | tf_op jit(solution)/shard_map/layer/pallas_call | solution.py:472
  60.0 2.1 %finish.1 = (bf16[2048,256]{1,0:T(8,128)(2,1)}, f32[256,256]{1,0:T(8,128)}) custom-call(bf16[2048,256]{1,0:T(8,128)(2,1)} %get-tuple-element.4.ing_in, f32[2,256,128]{2,1,0:T(8,128)} %get-tuple-element.5.wg_in), custom_call_target="tpu_custom_call" | custom-call | tf_op jit(solution)/shard_map/finish/pallas_call | solution.py:521
